TPU v7x, 32 devices: a whole 2x2x4 slice. The times are simulated.
32 devices in a mesh: row: 8 (over y, x, core), col: 4 (over z).
Axes of the slice: x: 2, y: 2, z: 4, core: 2. Of those that a mesh axis runs over, the one named last changes fastest.
Arguments:
- left_blocks: bfloat16 [8, 4, 64, 529], P('row', 'col'), may hold values from -1.1953125 to 1.1953125
- left_rows: int32 [8, 4, 64], P('row'), may hold values from 0 to 15
- left_cols: int32 [8, 4, 64], P('row'), may hold values from 0 to 15
- left_counts: int32 [8, 4], P('row'), may hold values from 32 to 64, as said below
- right_blocks: bfloat16 [8, 4, 128, 529], P('row', 'col'), may hold values from -6 to 6
- right_cols: int32 [8, 4, 16, 8], P(None, 'col'), may hold values from 0 to 31, as said below
Outputs:
- product: float32 [8, 4, 512, 529], P('row', 'col')
Inputs may be any that keep to these rules, and one draw needn't show every extreme that they name: `left_counts`: every count lies between 32 and 64, and some left panel is full in every draw. `right_cols`: the 8 block columns of one inner block row of one right panel are distinct.
All inputs are finite; a program needn't handle non-finite values.
Results may differ from a plain program's by a relative error of at most 0.0003.
Values may be sent and summed in bfloat16 or wider, within the bound.
No kernel may reach another device: no remote copies, remote signals or barrier semaphores. Data moves between devices by JAX's collectives and lax.ppermute only.
A program may use at most 64 MiB of HBM per device.

v0:
```python
import jax
import jax.numpy as jnp
from jax import lax
from jax.sharding import PartitionSpec as P

BS = 23
RB = 16
CB = 32
KB = 16
BPK = 8


def from_behind(value, axis, by):
    devices = lax.axis_size(axis)
    return lax.ppermute(value, axis, [(i, (i + by) % devices) for i in range(devices)])


def panel_products(blocks, rows, cols, count, kblocks, kcols):
    slots = blocks.shape[0]
    left_mats = blocks.reshape(slots, BS, BS)
    right_mats = kblocks.reshape(KB, BPK, BS, BS)[cols]
    products = jnp.einsum(
        "sij,srjk->srik", left_mats, right_mats, preferred_element_type=jnp.float32
    )
    keep = (jnp.arange(slots) < count).astype(jnp.float32)
    products = products * keep[:, None, None, None]
    target = rows[:, None] * CB + kcols[cols]
    return (products.reshape(slots * BPK, BS * BS), target.reshape(-1))


def body(left_blocks, left_rows, left_cols, left_counts, right_blocks, right_cols):
    ncol = lax.axis_size("col")
    nrow = lax.axis_size("row")
    col_index = lax.axis_index("col")
    row_index = lax.axis_index("row")
    lefts = [left_blocks]
    rights = [right_blocks]
    for offset in (1, 2):
        lefts.append(from_behind(lefts[-1], "col", -1))
        rights.append(from_behind(rights[-1], "row", -1))
    pieces = []
    for offset in range(3):
        panel = (col_index + offset) % ncol
        source = (row_index + offset) % nrow
        rows = lax.dynamic_index_in_dim(left_rows[0], panel, 0, keepdims=False)
        cols = lax.dynamic_index_in_dim(left_cols[0], panel, 0, keepdims=False)
        count = lax.dynamic_index_in_dim(left_counts[0], panel, 0, keepdims=False)
        kcols = lax.dynamic_index_in_dim(right_cols[:, 0], source, 0, keepdims=False)
        pieces.append(
            panel_products(lefts[offset][0, 0], rows, cols, count, rights[offset][0, 0], kcols)
        )
    total = jnp.zeros((RB * CB, BS * BS), jnp.float32)
    for products, target in pieces:
        total = total + jax.ops.segment_sum(products, target, num_segments=RB * CB)
    return total.reshape(1, 1, RB * CB, BS * BS)


def solution(mesh):
    in_specs = (
        P("row", "col", None, None),
        P("row", None, None),
        P("row", None, None),
        P("row", None),
        P("row", "col", None, None),
        P(None, "col", None, None),
    )
    out_specs = P("row", "col", None, None)
    return jax.shard_map(body, mesh=mesh, in_specs=in_specs, out_specs=out_specs, check_vma=False)
```

profile of v0, /device:TPU:0, one launch (start us, length us, event | category | flops | bytes accessed | tf_op | source)
XLA Modules:
  0.0 102.8 jit_solution(4959932037327749183)
XLA Ops:
  0.0 3.3 %collective-permute-start = (bf16[1,1,128,529]{2,3,1,0:T(8,128)(2,1)}, bf16[1,1,128,529]{2,3,1,0:T(8,128)(2,1)S(1)}, u32[]{:S(2)}, u32[]{:S(2)}) collective-permute-start(bf16[1,1,128,529]{2,3,1,0:T(8,128)(2,1)} %param.10), channel_id=1, source_target_pairs={{0,28},{4,0},{8,4},{12,8},{16,12},{20,16},{24,20},{28,24},{1,29},{... | collective-permute-start | bytes 406280 | tf_op jit(solution)/shard_map/ppermute | solution.py:15
  3.3 3.6 %collective-permute-start.1 = (bf16[1,1,64,529]{3,2,1,0:T(8,128)(2,1)}, bf16[1,1,64,529]{3,2,1,0:T(8,128)(2,1)}, u32[]{:S(2)}, u32[]{:S(2)}) collective-permute-start(bf16[1,1,64,529]{3,2,1,0:T(8,128)(2,1)} %param.6), channel_id=1, source_target_pairs={{0,3},{1,0},{2,1},{3,2},{4,7},{5,4},{6,5},{7,6},{8,11},{9,8},{10,9... | collective-permute-start | bytes 203144 | tf_op jit(solution)/shard_map/ppermute | solution.py:15
  6.9 1.1 %copy.11 = bf16[1,1,128,529]{3,2,1,0:T(8,128)(2,1)S(1)} copy(bf16[1,1,128,529]{2,3,1,0:T(8,128)(2,1)} %param.10) | data formatting | bytes 270848 | tf_op args[4]
  8.0 1.2 %reshape.304 = bf16[64,23,23,1]{2,1,0,3:T(8,128)(2,1)S(1)} reshape(bf16[1,1,64,529]{3,2,1,0:T(8,128)(2,1)} %param.6) | data formatting | bytes 135424 | tf_op jit(solution)/shard_map/reshape;squeeze | solution.py:20
  9.3 0.7 dynamic-slice_bitcast_fusion
  10.0 0.1 copy.10
  10.1 0.8 fusion.21
  10.9 0.8 fusion.29
  11.7 1.4 %constant_dynamic-slice_fusion = (s32[1,1]{1,0:T(1,128)}, s32[1,1]{1,0:T(1,128)}, s32[1,1]{1,0:T(1,128)}) fusion(s32[1,4]{1,0:T(1,128)} %param.9, s32[]{:T(128)S(6)} %select_n.98, s32[]{:T(128)S(6)} %select_n.88, s32[]{:T(128)S(6)} %select_n.93), kind=kLoop, calls=%fused_computation.34 | loop fusion | bytes 36 | tf_op jit(solution)/shard_map/jit(dynamic_index_in_dim)/dynamic_slice | solution.py:47
  13.0 0.6 compare_convert_fusion.2
  13.7 0.6 reshape_squeeze.18
  14.4 0.1 copy.12
  14.5 0.6 gather_fusion
  15.1 2.6 %gather_fusion.1 = bf16[64,8,23,23]{3,1,2,0:T(8,128)(2,1)} fusion(bf16[16,8,23,23]{3,1,2,0:T(8,128)(2,1)S(1)} %copy.12, s32[1024]{0:T(1024)S(1)} %pad_clamp_fusion.2), kind=kCustom, calls=%fused_computation.1 | custom fusion | bytes 1083648 | tf_op jit(solution)/shard_map/gather | solution.py:21
  17.7 0.1 copy.24
  17.7 0.1 copy.17
  17.8 0.0 copy-start
  17.8 0.1 broadcast_add_fusion.2
  17.9 0.6 gather_fusion.4
  18.5 0.6 gather_fusion.2
  19.1 5.9 %multiply_bitcast_fusion.2 = f32[64,8,23,23]{2,3,1,0:T(8,128)} fusion(f32[64]{0:T(128)S(1)} %compare_convert_fusion.2, bf16[64,8,23,23]{3,1,2,0:T(8,128)(2,1)} %gather_fusion.1, bf16[64,23,23,1]{2,1,0,3:T(8,128)(2,1)S(1)} %reshape.304), kind=kOutput, calls=%fused_computation.11 | convolution fusion | flops 12729856 | bytes 1693056 | tf_op jit(solution)/shard_map/sij,srjk->srik/dot_general | solution.py:22
  25.0 0.0 copy-done
  25.0 0.1 broadcast_add_fusion
  25.1 1.2 %compare_convert_fusion.1 = f32[64]{0:T(128)} fusion(s32[]{:T(128)} %bitcast.12), kind=kLoop, calls=%fused_computation.47 | loop fusion | flops 128 | bytes 260 | tf_op jit(solution)/shard_map/convert_element_type | solution.py:25
  26.3 0.1 reshape.279
  26.4 7.5 %copy.16 = f32[64,8,23,23]{3,2,1,0:T(8,128)} copy(f32[64,8,23,23]{2,3,1,0:T(8,128)} %multiply_bitcast_fusion.2) | data formatting | bytes 2166784 | tf_op jit(solution)/shard_map/mul | solution.py:26
  33.9 4.3 %reshape.281 = f32[512,529]{1,0:T(8,128)S(1)} reshape(f32[64,8,23,23]{3,2,1,0:T(8,128)} %copy.16) | data formatting | bytes 2166784 | tf_op jit(solution)/shard_map/reshape | solution.py:28
  38.2 0.6 reshape.287
  38.9 0.1 reshape.295
  39.0 4.2 %scatter_custom_fusion = f32[512,529]{1,0:T(8,128)S(1)} fusion(s32[512]{0:T(512)S(1)} %reshape.279, f32[512,529]{1,0:T(8,128)S(1)} %reshape.281, f32[]{:T(128)} %constant.88.clone.1), kind=kCustom, calls=%fused_computation.20 | custom fusion | flops 270848 | bytes 1083396 | tf_op jit(solution)/shard_map/scatter-add | solution.py:54
  43.1 1.1 %compare_convert_fusion = f32[64]{0:T(128)} fusion(s32[]{:T(128)} %bitcast.19), kind=kLoop, calls=%fused_computation.46 | loop fusion | flops 128 | bytes 260 | tf_op jit(solution)/shard_map/convert_element_type | solution.py:25
  44.2 0.0 collective-permute-done.1
  44.2 1.2 %reshape.305 = bf16[64,23,23,1]{2,1,0,3:T(8,128)(2,1)S(1)} reshape(bf16[1,1,64,529]{3,2,1,0:T(8,128)(2,1)} %collective-permute-done.1) | data formatting | bytes 135424 | tf_op jit(solution)/shard_map/reshape;squeeze | solution.py:20
  45.5 0.5 collective-permute-start.3
  46.0 0.0 collective-permute-done
  46.0 0.2 copy.18
  46.1 0.7 reshape_squeeze.20
  46.8 0.1 copy.19
  46.9 0.0 copy-start.2
  46.9 2.7 %gather_fusion.3 = bf16[64,8,23,23]{3,1,2,0:T(8,128)(2,1)} fusion(bf16[16,8,23,23]{3,1,2,0:T(8,128)(2,1)S(1)} %copy.19, s32[1024]{0:T(1024)} %copy-done), kind=kCustom, calls=%fused_computation.3 | custom fusion | bytes 1083648 | tf_op jit(solution)/shard_map/gather | solution.py:21
  49.6 0.1 collective-permute-start.2
  49.7 0.0 copy-done.2
  49.7 5.9 %multiply_bitcast_fusion.1 = f32[64,8,23,23]{2,3,1,0:T(8,128)} fusion(f32[64]{0:T(128)S(1)} %copy-done.2, bf16[64,8,23,23]{3,1,2,0:T(8,128)(2,1)} %gather_fusion.3, bf16[64,23,23,1]{2,1,0,3:T(8,128)(2,1)S(1)} %reshape.305), kind=kOutput, calls=%fused_computation.10 | convolution fusion | flops 12729856 | bytes 1693056 | tf_op jit(solution)/shard_map/sij,srjk->srik/dot_general | solution.py:22
  55.6 7.5 %copy.23 = f32[64,8,23,23]{3,2,1,0:T(8,128)} copy(f32[64,8,23,23]{2,3,1,0:T(8,128)} %multiply_bitcast_fusion.1) | data formatting | bytes 2166784 | tf_op jit(solution)/shard_map/mul | solution.py:26
  63.2 4.3 %reshape.289 = f32[512,529]{1,0:T(8,128)S(1)} reshape(f32[64,8,23,23]{3,2,1,0:T(8,128)} %copy.23) | data formatting | bytes 2166784 | tf_op jit(solution)/shard_map/reshape | solution.py:28
  67.5 5.1 %scatter_custom_fusion.1 = f32[512,529]{1,0:T(8,128)} fusion(s32[512]{0:T(512)} %reshape.287, f32[512,529]{1,0:T(8,128)S(1)} %reshape.289, f32[]{:T(128)} %constant.88.clone.1), kind=kCustom, calls=%fused_computation.18 | custom fusion | flops 270848 | bytes 1083904 | tf_op jit(solution)/shard_map/scatter-add | solution.py:54
  72.5 1.4 %add.174 = f32[512,529]{1,0:T(8,128)S(1)} add(f32[512,529]{1,0:T(8,128)S(1)} %scatter_custom_fusion, f32[512,529]{1,0:T(8,128)} %scatter_custom_fusion.1) | non-fusion elementwise | flops 270848 | bytes 3250176 | tf_op jit(solution)/shard_map/add | solution.py:54
  74.0 0.0 collective-permute-done.3
  74.0 1.2 %reshape.306 = bf16[64,23,23,1]{2,1,0,3:T(8,128)(2,1)S(1)} reshape(bf16[1,1,64,529]{3,2,1,0:T(8,128)(2,1)} %collective-permute-done.3) | data formatting | bytes 135424 | tf_op jit(solution)/shard_map/reshape;squeeze | solution.py:20
  75.2 0.0 collective-permute-done.2
  75.2 0.2 copy.25
  75.4 0.7 reshape_squeeze.22
  76.1 0.1 copy.26
  76.2 0.0 copy-start.1
  76.2 2.6 %gather_fusion.5 = bf16[64,8,23,23]{3,1,2,0:T(8,128)(2,1)} fusion(bf16[16,8,23,23]{3,1,2,0:T(8,128)(2,1)S(1)} %copy.26, s32[1024]{0:T(1024)S(1)} %pad_clamp_fusion), kind=kCustom, calls=%fused_computation.5 | custom fusion | bytes 1083648 | tf_op jit(solution)/shard_map/gather | solution.py:21
  78.8 0.0 copy-done.1
  78.8 5.9 %multiply_bitcast_fusion = f32[64,8,23,23]{2,3,1,0:T(8,128)} fusion(f32[64]{0:T(128)S(1)} %copy-done.1, bf16[64,8,23,23]{3,1,2,0:T(8,128)(2,1)} %gather_fusion.5, bf16[64,23,23,1]{2,1,0,3:T(8,128)(2,1)S(1)} %reshape.306), kind=kOutput, calls=%fused_computation.9 | convolution fusion | flops 12729856 | bytes 1693056 | tf_op jit(solution)/shard_map/sij,srjk->srik/dot_general | solution.py:22
  84.7 7.5 %copy.30 = f32[64,8,23,23]{3,2,1,0:T(8,128)} copy(f32[64,8,23,23]{2,3,1,0:T(8,128)} %multiply_bitcast_fusion) | data formatting | bytes 2166784 | tf_op jit(solution)/shard_map/mul | solution.py:26
  92.2 4.3 %reshape.297 = f32[512,529]{1,0:T(8,128)S(1)} reshape(f32[64,8,23,23]{3,2,1,0:T(8,128)} %copy.30) | data formatting | bytes 2166784 | tf_op jit(solution)/shard_map/reshape | solution.py:28
  96.5 4.4 %scatter_fusion = f32[512,529]{1,0:T(8,128)S(1)} fusion(f32[512,529]{1,0:T(8,128)S(1)} %add.174, s32[512]{0:T(512)S(1)} %reshape.295, f32[512,529]{1,0:T(8,128)S(1)} %reshape.297), kind=kCustom, calls=%fused_computation.8 | custom fusion | flops 270848 | bytes 3252224 | tf_op jit(solution)/shard_map/scatter-add | solution.py:54
  100.9 2.0 %copy.31 = f32[1,1,512,529]{2,1,3,0:T(1,128)} copy(f32[1,1,512,529]{3,2,1,0:T(8,128)S(1)} %bitcast.61) | data formatting | bytes 2166784 | tf_op jit(solution)/shard_map/reshape | solution.py:55
  (3 shorter events, 0.0 us)
Async XLA Ops:
  0.0 46.0 %collective-permute-start = (bf16[1,1,128,529]{2,3,1,0:T(8,128)(2,1)}, bf16[1,1,128,529]{2,3,1,0:T(8,128)(2,1)S(1)}, u32[]{:S(2)}, u32[]{:S(2)}) collective-permute-start(bf16[1,1,128,529]{2,3,1,0:T(8,128)(2,1)} %param.10), channel_id=1, source_target_pairs={{0,28},{4,0},{8,4},{12,8},{16,12},{20,16},{24,20},{28,24},{1,29},{... | collective-permute-start | bytes 406280 | tf_op jit(solution)/shard_map/ppermute | solution.py:15
  3.3 40.9 %collective-permute-start.1 = (bf16[1,1,64,529]{3,2,1,0:T(8,128)(2,1)}, bf16[1,1,64,529]{3,2,1,0:T(8,128)(2,1)}, u32[]{:S(2)}, u32[]{:S(2)}) collective-permute-start(bf16[1,1,64,529]{3,2,1,0:T(8,128)(2,1)} %param.6), channel_id=1, source_target_pairs={{0,3},{1,0},{2,1},{3,2},{4,7},{5,4},{6,5},{7,6},{8,11},{9,8},{10,9... | collective-permute-start | bytes 203144 | tf_op jit(solution)/shard_map/ppermute | solution.py:15
  17.8 7.2 %copy-start = (s32[1024]{0:T(1024)}, s32[1024]{0:T(1024)S(1)}, u32[]{:S(2)}) copy-start(s32[1024]{0:T(1024)S(1)} %pad_clamp_fusion.1) | copy-start | bytes 12292
  45.5 28.5 %collective-permute-start.3 = (bf16[1,1,64,529]{3,2,1,0:T(8,128)(2,1)}, bf16[1,1,64,529]{3,2,1,0:T(8,128)(2,1)}, u32[]{:S(2)}, u32[]{:S(2)}) collective-permute-start(bf16[1,1,64,529]{3,2,1,0:T(8,128)(2,1)} %collective-permute-done.1), channel_id=1, source_target_pairs={{0,3},{1,0},{2,1},{3,2},{4,7},{5,4},{6,5},{7,6},{8,11},{9,8},{10,9... | collective-permute-start | bytes 203144 | tf_op jit(solution)/shard_map/ppermute | solution.py:15
  46.9 2.8 %copy-start.2 = (f32[64]{0:T(128)S(1)}, f32[64]{0:T(128)}, u32[]{:S(2)}) copy-start(f32[64]{0:T(128)} %compare_convert_fusion.1) | copy-start | bytes 772
  49.6 25.6 %collective-permute-start.2 = (bf16[1,1,128,529]{2,3,1,0:T(8,128)(2,1)S(1)}, bf16[1,1,128,529]{2,3,1,0:T(8,128)(2,1)S(1)}, u32[]{:S(2)}, u32[]{:S(2)}) collective-permute-start(bf16[1,1,128,529]{2,3,1,0:T(8,128)(2,1)S(1)} %collective-permute-done), channel_id=1, source_target_pairs={{0,28},{4,0},{8,4},{12,8},{16,12},{20,16},{24,20},{28,24},{1,29},{... | collective-permute-start | bytes 406280 | tf_op jit(solution)/shard_map/ppermute | solution.py:15
  76.2 2.6 %copy-start.1 = (f32[64]{0:T(128)S(1)}, f32[64]{0:T(128)}, u32[]{:S(2)}) copy-start(f32[64]{0:T(128)} %compare_convert_fusion) | copy-start | bytes 772
where the time goes:
time: 104 us; the launch traced here: 103 us
  local copies, waits for them, and re-layouts  57.6 us (55%)
  other arithmetic  19.8 us (19%)
  matrix products  17.7 us (17%)
  starting transfers between devices  7.55 us (7%)
    mul x3, local copies, waits for them, and re-layouts, panel_products(): products = products * keep[:, None, None, None]  22.5 us
    dot_general x3, matrix products, panel_products(): jnp.einsum('sij,srjk->srik', left_mats, right_mats, preferred_element_typ...  17.7 us
    scatter-add x3, other arithmetic, body(): total = total + jax.ops.segment_sum(products, target, num_segments=RB * CB)  13.6 us
    reshape x3, local copies, waits for them, and re-layouts, panel_products(): return (products.reshape(slots * BPK, BS * BS), target.reshape(-1))  12.9 us
    gather x3, local copies, waits for them, and re-layouts, panel_products(): right_mats = kblocks.reshape(KB, BPK, BS, BS)[cols]  7.91 us
    ppermute x4, starting transfers between devices, from_behind(): lax.ppermute(value, axis, [(i, (i + by) % devices) for i in range(devices)])  7.55 us
    another operation x3, local copies, waits for them, and re-layouts, panel_products(): left_mats = blocks.reshape(slots, BS, BS)  3.71 us
    convert_element_type x3, other arithmetic, panel_products(): keep = (jnp.arange(slots) < count).astype(jnp.float32)  2.96 us
  transfers between devices with their start and end apart: 4, of which 0 were waited for; matrix products, arithmetic and copies ran while one was open for 66% of the time, Pallas kernels for 0%

commit v1 on v0

v1 whole, which is shorter than its diff:
```python
import functools
import jax
import jax.numpy as jnp
from jax import lax
from jax.experimental import pallas as pl
from jax.experimental.pallas import tpu as pltpu
from jax.sharding import PartitionSpec as P

BS = 23
RB = 16
CB = 32
KB = 16
BPK = 8
SA = 64
JP = 32
QUADS = 6
NB = BS * BS
F32 = jnp.float32
BF16 = jnp.bfloat16


def from_behind(value, axis, by):
    devices = lax.axis_size(axis)
    return lax.ppermute(value, axis, [(i, (i + by) % devices) for i in range(devices)])


def swap_quads(v):
    lane = lax.broadcasted_iota(jnp.int32, v[0].shape, 1)
    half = lane < 64
    even = (lane & 32) == 0
    w = [None] * 4
    for a in (0, 1):
        w[a] = jnp.where(half, v[a], pltpu.roll(v[a + 2], 64, 1))
        w[a + 2] = jnp.where(half, pltpu.roll(v[a], 64, 1), v[a + 2])
    z = [None] * 4
    for a in (0, 2):
        z[a] = jnp.where(even, w[a], pltpu.roll(w[a + 1], 32, 1))
        z[a + 1] = jnp.where(even, pltpu.roll(w[a], 96, 1), w[a + 1])
    return z


def spread_matrix(t_ref):
    lane = lax.broadcasted_iota(jnp.int32, (1, QUADS * 128), 1)
    i, j = lane >> 5, lane & 31
    source = jnp.where((j < BS) & (i < BS), i * BS + j, -1)
    entry = lax.broadcasted_iota(jnp.int32, (NB, QUADS * 128), 0)
    t_ref[...] = jnp.where(entry == source, 1.0, 0.0).astype(BF16)


def left_panel(blocks, rows, cols, count, t_ref, a_ref, base):
    wide = jnp.dot(blocks, t_ref[...], preferred_element_type=F32).astype(BF16)
    slot = lax.broadcasted_iota(jnp.int32, (1, SA), 1)
    code = jnp.where(slot < count, cols * RB + rows, -1)
    place = lax.broadcasted_iota(jnp.int32, (KB * RB, SA), 0)
    pick = jnp.where(place == code, 1.0, 0.0).astype(BF16)
    for q in range(QUADS):
        sums = jnp.dot(pick, wide[:, q * 128 : (q + 1) * 128], preferred_element_type=F32)
        for g in range(KB // 4):
            v = [sums[(4 * g + a) * RB : (4 * g + a + 1) * RB] for a in range(4)]
            for a, z in enumerate(swap_quads(v)):
                i = 4 * q + a
                if i < BS:
                    hi = z.astype(BF16)
                    lo = (z - hi.astype(F32)).astype(BF16)
                    at = base + g * 128
                    a_ref[i * RB : (i + 1) * RB, at : at + 128] = hi
                    a_ref[(BS + i) * RB : (BS + i + 1) * RB, at : at + 128] = lo


def right_panel(blocks, cols, w_ref, b_ref, base):
    w_ref[528:552, :] = jnp.zeros((24, 128), F32)
    w_ref[0:NB, :] = blocks.astype(F32)
    lane = lax.broadcasted_iota(jnp.int32, (BPK, 128), 1)
    none = jnp.zeros((BPK, 128), F32)
    spread = []
    for kap in range(KB):
        one = jnp.where(lane - 32 * (kap % 4) == cols[:, kap : kap + 1], 1.0, 0.0)
        spread.append(jnp.concatenate([one if g == kap // 4 else none for g in range(4)], axis=1))
    spread = jnp.concatenate(spread, axis=0).astype(BF16)
    pad = jnp.zeros((8, 128), F32)
    for q in range(QUADS):
        entries = []
        for a in range(4):
            k = 4 * q + a
            if k < BS:
                entries += [w_ref[pl.ds(k, 24, stride=BS), :], pad]
            else:
                entries += [pad] * 4
        entries = jnp.concatenate(entries, axis=0).astype(BF16)
        full = jnp.dot(entries, spread, preferred_element_type=F32)
        for g in range(4):
            v = [full[a * JP : (a + 1) * JP, g * 128 : (g + 1) * 128] for a in range(4)]
            for a, z in enumerate(swap_quads(v)):
                at = base + (4 * g + a) * JP
                b_ref[at : at + JP, q * 128 : (q + 1) * 128] = z.astype(BF16)


def kernel(counts_ref, l0, l1, l2, rows_ref, cols_ref, r0, r1, r2, kcols_ref, out_ref,
           t_ref, a_ref, w_ref, b_ref, p_ref):
    ncol, nrow = rows_ref.shape[1], kcols_ref.shape[0]
    spread_matrix(t_ref)
    for s, (l, r) in enumerate(((l0, r0), (l1, r1), (l2, r2))):
        panel = lax.rem(lax.axis_index("col") + s, ncol)
        source = lax.rem(lax.axis_index("row") + s, nrow)
        rows = rows_ref[0, pl.ds(panel, 1), :]
        cols = cols_ref[0, pl.ds(panel, 1), :]
        left_panel(l[...], rows, cols, counts_ref[0, panel], t_ref, a_ref, s * 512)
        right_panel(r[...], kcols_ref[source], w_ref, b_ref, s * 512)
    for q in range(QUADS):
        lanes = slice(q * 128, (q + 1) * 128)
        both = jnp.dot(a_ref[...], b_ref[:, lanes], preferred_element_type=F32)
        for i in range(BS):
            total = both[i * RB : (i + 1) * RB] + both[(BS + i) * RB : (BS + i + 1) * RB]
            p_ref[q, pl.ds(i, RB, stride=24), :] = total
    for rq in range(RB // 4):
        for ib in range(3):
            for q in range(QUADS):
                v = [p_ref[q, (4 * rq + a) * 24 + ib * 8 : (4 * rq + a) * 24 + ib * 8 + 8, :] for a in range(4)]
                for a, z in enumerate(swap_quads(v)):
                    k = 4 * q + a
                    n = 8 if ib < 2 else 7
                    if k < BS:
                        out_ref[pl.ds((ib * 8 * BS + k) * 4 + rq, n, stride=4 * BS), :] = z[:n]


def body(left_blocks, left_rows, left_cols, left_counts, right_blocks, right_cols):
    left = left_blocks[0, 0]
    right = jnp.swapaxes(right_blocks[0, 0], 0, 1)
    kcols = jnp.swapaxes(right_cols[:, 0], 1, 2)
    l1, l2 = from_behind(left, "col", -1), from_behind(left, "col", -2)
    r1, r2 = from_behind(right, "row", -1), from_behind(right, "row", -2)
    vmem = pl.BlockSpec(memory_space=pltpu.VMEM)
    out = pl.pallas_call(
        kernel,
        out_shape=jax.ShapeDtypeStruct((NB * 4, 128), F32),
        in_specs=[pl.BlockSpec(memory_space=pltpu.SMEM)] + [vmem] * 9,
        out_specs=vmem,
        scratch_shapes=[
            pltpu.VMEM((NB, QUADS * 128), BF16),
            pltpu.VMEM((2 * BS * RB, 3 * 512), BF16),
            pltpu.VMEM((552, 128), F32),
            pltpu.VMEM((3 * 512, QUADS * 128), BF16),
            pltpu.VMEM((QUADS, RB * 24, 128), F32),
        ],
        compiler_params=pltpu.CompilerParams(vmem_limit_bytes=32 * 1024 * 1024),
    )(left_counts, left, l1, l2, left_rows, left_cols, right, r1, r2, kcols)
    return jnp.swapaxes(out.reshape(NB, RB * CB), 0, 1)[None, None]


def solution(mesh):
    in_specs = (
        P("row", "col", None, None),
        P("row", None, None),
        P("row", None, None),
        P("row", None),
        P("row", "col", None, None),
        P(None, "col", None, None),
    )
    out_specs = P("row", "col", None, None)
    return jax.shard_map(body, mesh=mesh, in_specs=in_specs, out_specs=out_specs, check_vma=False)
```

time: 104 us -> 25.2 us (0.24)
  local copies, waits for them, and re-layouts: 57.6 us -> 6.45 us
  other arithmetic: 19.8 us -> 0 us
  matrix products: 17.7 us -> 0 us
  Pallas kernels: 0 us -> 6.39 us
  waiting for transfers between devices: 0.01 us -> 4.17 us
    mul x3 -> x0, local copies, waits for them, and re-layouts: 22.5 us -> none  [panel_products(): products = products * keep[:, None, None, None]]
    dot_general x3 -> x0, matrix products: 17.7 us -> none  [panel_products(): jnp.einsum('sij,srjk->srik', left_mats, right_mats, preferred_element_typ...]
    reshape x4 -> x1, local copies, waits for them, and re-layouts: 14.9 us -> 0.16 us  [body(): return jnp.swapaxes(out.reshape(NB, RB * CB), 0, 1)[None, None]]
    scatter-add x3 -> x0, other arithmetic: 13.6 us -> none  [body(): total = total + jax.ops.segment_sum(products, target, num_segments=RB * CB)]
    gather x6 -> x0, local copies, waits for them, and re-layouts: 9.7 us -> none  [the longest x3 7.91 us: panel_products(): right_mats = kblocks.reshape(KB, BPK, BS, BS)[cols]]
    pallas_call x0 -> x1, Pallas kernels: none -> 6.39 us  [body(): pl.pallas_call(kernel, out_shape=jax.ShapeDtypeStruct((NB * 4, 128), F32)...]
    another operation x9 -> x0, local copies, waits for them, and re-layouts: 5.96 us -> none  [the longest x3 3.71 us: panel_products(): left_mats = blocks.reshape(slots, BS, BS)]
    ppermute x4, waiting for transfers between devices: 0.01 us -> 4.17 us  [from_behind(): lax.ppermute(value, axis, [(i, (i + by) % devices) for i in range(devices)])]
  transfers between devices with their start and end apart: 4 -> 4, of which waited for: 0 -> 1; matrix products, arithmetic and copies ran while one was open for 66% -> 0% of each run, Pallas kernels for 0% -> 0%
where the time goes in v1:
time: 25.2 us; the launch traced here: 24.9 us
  starting transfers between devices  7.83 us (31%)
  local copies, waits for them, and re-layouts  6.45 us (26%)
  Pallas kernels  6.39 us (25%)
  waiting for transfers between devices  4.17 us (17%)
    ppermute x4, starting transfers between devices, from_behind(): lax.ppermute(value, axis, [(i, (i + by) % devices) for i in range(devices)])  7.83 us
    pallas_call x1, Pallas kernels, body(): pl.pallas_call(kernel, out_shape=jax.ShapeDtypeStruct((NB * 4, 128), F32)...  6.39 us
    unnamed x12, local copies, waits for them, and re-layouts  4.56 us
    ppermute x4, waiting for transfers between devices, from_behind(): lax.ppermute(value, axis, [(i, (i + by) % devices) for i in range(devices)])  4.17 us
    broadcast_in_dim x1, local copies, waits for them, and re-layouts, body(): return jnp.swapaxes(out.reshape(NB, RB * CB), 0, 1)[None, None]  1.73 us
  transfers between devices with their start and end apart: 4, of which 1 were waited for; matrix products, arithmetic and copies ran while one was open for 0% of the time, Pallas kernels for 0%

profile of v1, /device:TPU:0, one launch (start us, length us, event | category | flops | bytes accessed | tf_op | source)
XLA Modules:
  0.0 24.9 jit_solution(13552015349362648785)
XLA Ops:
  0.0 3.9 %collective-permute-start.3 = (bf16[529,128]{1,0:T(8,128)(2,1)}, bf16[529,128]{1,0:T(8,128)(2,1)S(1)}, u32[]{:S(2)}, u32[]{:S(2)}) collective-permute-start(bf16[529,128]{1,0:T(8,128)(2,1)} %bitcast.10), channel_id=1, source_target_pairs={{0,24},{4,28},{8,0},{12,4},{16,8},{20,12},{24,16},{28,20},{1,25},{... | collective-permute-start | bytes 406280 | tf_op jit(solution)/shard_map/ppermute | solution.py:24
  3.9 0.0 collective-permute-start.2
  3.9 2.6 %collective-permute-start.1 = (bf16[64,529]{1,0:T(8,128)(2,1)}, bf16[64,529]{1,0:T(8,128)(2,1)S(1)}, u32[]{:S(2)}, u32[]{:S(2)}) collective-permute-start(bf16[64,529]{1,0:T(8,128)(2,1)} %bitcast.13), channel_id=1, source_target_pairs={{0,2},{1,3},{2,0},{3,1},{4,6},{5,7},{6,4},{7,5},{8,10},{9,11},{10,... | collective-permute-start | bytes 203144 | tf_op jit(solution)/shard_map/ppermute | solution.py:24
  6.5 1.3 %collective-permute-start = (bf16[64,529]{1,0:T(8,128)(2,1)}, bf16[64,529]{1,0:T(8,128)(2,1)S(1)}, u32[]{:S(2)}, u32[]{:S(2)}) collective-permute-start(bf16[64,529]{1,0:T(8,128)(2,1)} %bitcast.14), channel_id=1, source_target_pairs={{0,3},{1,0},{2,1},{3,2},{4,7},{5,4},{6,5},{7,6},{8,11},{9,8},{10,9... | collective-permute-start | bytes 203144 | tf_op jit(solution)/shard_map/ppermute | solution.py:24
  7.8 4.2 %collective-permute-done.1.l2 = bf16[64,529]{1,0:T(8,128)(2,1)S(1)} collective-permute-done((bf16[64,529]{1,0:T(8,128)(2,1)}, bf16[64,529]{1,0:T(8,128)(2,1)S(1)}, u32[]{:S(2)}, u32[]{:S(2)}) %collective-permute-start.1) | collective-permute-done | bytes 67744 | tf_op jit(solution)/shard_map/ppermute | solution.py:24
  12.0 0.0 collective-permute-done.l1
  12.0 0.0 collective-permute-done.3.r2
  12.0 0.0 collective-permute-done.2.r1
  12.0 0.0 copy-start
  12.0 0.9 %copy-done = bf16[1,1,128,529]{2,3,1,0:T(8,128)(2,1)S(1)} copy-done((bf16[1,1,128,529]{2,3,1,0:T(8,128)(2,1)S(1)}, bf16[1,1,128,529]{2,3,1,0:T(8,128)(2,1)}, u32[]{:S(2)}) %copy-start) | copy-done | bytes 135448
  12.9 0.0 copy-start.1
  12.9 0.9 %copy-done.1 = bf16[1,1,64,529]{3,2,1,0:T(8,128)(2,1)S(1)} copy-done((bf16[1,1,64,529]{3,2,1,0:T(8,128)(2,1)S(1)}, bf16[1,1,64,529]{3,2,1,0:T(8,128)(2,1)}, u32[]{:S(2)}) %copy-start.1) | copy-done | bytes 67736
  13.8 0.0 copy-start.2
  13.8 0.8 %copy-done.2 = s32[8,1,16,8]{2,3,1,0:T(8,128)S(1)} copy-done((s32[8,1,16,8]{2,3,1,0:T(8,128)S(1)}, s32[8,1,16,8]{2,3,1,0:T(8,128)}, u32[]{:S(2)}) %copy-start.2) | copy-done | bytes 4120
  14.6 0.0 copy-start.3
  14.6 0.7 %copy-done.3 = s32[1,4,64]{2,1,0:T(4,128)S(1)} copy-done((s32[1,4,64]{2,1,0:T(4,128)S(1)}, s32[1,4,64]{2,1,0:T(4,128)}, u32[]{:S(2)}) %copy-start.3) | copy-done | bytes 1048
  15.3 0.0 copy-start.4
  15.3 0.7 %copy-done.4 = s32[1,4,64]{2,1,0:T(4,128)S(1)} copy-done((s32[1,4,64]{2,1,0:T(4,128)S(1)}, s32[1,4,64]{2,1,0:T(4,128)}, u32[]{:S(2)}) %copy-start.4) | copy-done | bytes 1048
  15.9 0.0 copy-start.5
  15.9 0.7 %copy-done.5 = s32[1,4]{1,0:T(1,128)S(1)} copy-done((s32[1,4]{1,0:T(1,128)S(1)}, s32[1,4]{1,0:T(1,128)}, u32[]{:S(2)}) %copy-start.5) | copy-done | bytes 40
  16.6 6.4 %shard_map.64 = f32[2116,128]{1,0:T(8,128)S(1)} custom-call(s32[1,4]{1,0:T(1,128)S(1)} %copy-done.5, bf16[64,529]{1,0:T(8,128)(2,1)S(1)} %bitcast.15, bf16[64,529]{1,0:T(8,128)(2,1)S(1)} %collective-permute-done.l1, bf16[64,529]{1,0:T(8,128)(2,1)S(1)} %collective-permute-done.1.l2, s32[1,4,64]{2,1,0:T(4,128)S(1)} %copy-done.3, s32[1,4,64]{2,1,0:T(4,128)S(1)} %copy-done.4, ...), custom_call_target="tpu_custom_call" | custom-call | tf_op jit(solution)/shard_map/pallas_call | solution.py:133
  23.0 0.2 reshape.3
  23.2 1.7 %broadcast_in_dim.3 = f32[1,1,512,529]{2,1,3,0:T(1,128)} reshape(f32[512,529]{0,1:T(8,128)S(1)} %bitcast.17) | data formatting | bytes 2166784 | tf_op jit(solution)/shard_map/broadcast_in_dim | solution.py:147
Async XLA Ops:
  0.0 12.0 %collective-permute-start.3 = (bf16[529,128]{1,0:T(8,128)(2,1)}, bf16[529,128]{1,0:T(8,128)(2,1)S(1)}, u32[]{:S(2)}, u32[]{:S(2)}) collective-permute-start(bf16[529,128]{1,0:T(8,128)(2,1)} %bitcast.10), channel_id=1, source_target_pairs={{0,24},{4,28},{8,0},{12,4},{16,8},{20,12},{24,16},{28,20},{1,25},{... | collective-permute-start | bytes 406280 | tf_op jit(solution)/shard_map/ppermute | solution.py:24
  3.9 8.1 %collective-permute-start.2 = (bf16[529,128]{1,0:T(8,128)(2,1)}, bf16[529,128]{1,0:T(8,128)(2,1)S(1)}, u32[]{:S(2)}, u32[]{:S(2)}) collective-permute-start(bf16[529,128]{1,0:T(8,128)(2,1)} %bitcast.11), channel_id=1, source_target_pairs={{0,28},{4,0},{8,4},{12,8},{16,12},{20,16},{24,20},{28,24},{1,29},{... | collective-permute-start | bytes 406280 | tf_op jit(solution)/shard_map/ppermute | solution.py:24
  3.9 8.1 %collective-permute-start.1 = (bf16[64,529]{1,0:T(8,128)(2,1)}, bf16[64,529]{1,0:T(8,128)(2,1)S(1)}, u32[]{:S(2)}, u32[]{:S(2)}) collective-permute-start(bf16[64,529]{1,0:T(8,128)(2,1)} %bitcast.13), channel_id=1, source_target_pairs={{0,2},{1,3},{2,0},{3,1},{4,6},{5,7},{6,4},{7,5},{8,10},{9,11},{10,... | collective-permute-start | bytes 203144 | tf_op jit(solution)/shard_map/ppermute | solution.py:24
  6.5 5.5 %collective-permute-start = (bf16[64,529]{1,0:T(8,128)(2,1)}, bf16[64,529]{1,0:T(8,128)(2,1)S(1)}, u32[]{:S(2)}, u32[]{:S(2)}) collective-permute-start(bf16[64,529]{1,0:T(8,128)(2,1)} %bitcast.14), channel_id=1, source_target_pairs={{0,3},{1,0},{2,1},{3,2},{4,7},{5,4},{6,5},{7,6},{8,11},{9,8},{10,9... | collective-permute-start | bytes 203144 | tf_op jit(solution)/shard_map/ppermute | solution.py:24
  12.0 0.9 %copy-start = (bf16[1,1,128,529]{2,3,1,0:T(8,128)(2,1)S(1)}, bf16[1,1,128,529]{2,3,1,0:T(8,128)(2,1)}, u32[]{:S(2)}) copy-start(bf16[1,1,128,529]{2,3,1,0:T(8,128)(2,1)} %param.10) | copy-start | bytes 406276
  12.9 0.9 %copy-start.1 = (bf16[1,1,64,529]{3,2,1,0:T(8,128)(2,1)S(1)}, bf16[1,1,64,529]{3,2,1,0:T(8,128)(2,1)}, u32[]{:S(2)}) copy-start(bf16[1,1,64,529]{3,2,1,0:T(8,128)(2,1)} %param.6) | copy-start | bytes 203140
  13.8 0.8 %copy-start.2 = (s32[8,1,16,8]{2,3,1,0:T(8,128)S(1)}, s32[8,1,16,8]{2,3,1,0:T(8,128)}, u32[]{:S(2)}) copy-start(s32[8,1,16,8]{2,3,1,0:T(8,128)} %param.11) | copy-start | bytes 12292
  14.6 0.7 %copy-start.3 = (s32[1,4,64]{2,1,0:T(4,128)S(1)}, s32[1,4,64]{2,1,0:T(4,128)}, u32[]{:S(2)}) copy-start(s32[1,4,64]{2,1,0:T(4,128)} %rows_ref.1) | copy-start | bytes 3076
  15.3 0.7 %copy-start.4 = (s32[1,4,64]{2,1,0:T(4,128)S(1)}, s32[1,4,64]{2,1,0:T(4,128)}, u32[]{:S(2)}) copy-start(s32[1,4,64]{2,1,0:T(4,128)} %cols_ref.1) | copy-start | bytes 3076
  15.9 0.7 %copy-start.5 = (s32[1,4]{1,0:T(1,128)S(1)}, s32[1,4]{1,0:T(1,128)}, u32[]{:S(2)}) copy-start(s32[1,4]{1,0:T(1,128)} %counts_ref.1) | copy-start | bytes 52

commit v2 on v1

v2 whole, which is shorter than its diff:
```python
import functools
import jax
import jax.numpy as jnp
from jax import lax
from jax.experimental import pallas as pl
from jax.experimental.pallas import tpu as pltpu
from jax.sharding import PartitionSpec as P

BS = 23
RB = 16
CB = 32
KB = 16
BPK = 8
SA = 64
JP = 32
QUADS = 6
NB = BS * BS
WIDE = QUADS * 128
DEPTH = KB * JP
F32 = jnp.float32
BF16 = jnp.bfloat16


def from_behind(value, axis, by):
    devices = lax.axis_size(axis)
    return lax.ppermute(value, axis, [(i, (i + by) % devices) for i in range(devices)])


def swap_quads(v):
    lane = lax.broadcasted_iota(jnp.int32, v[0].shape, 1)
    half = lane < 64
    even = (lane & 32) == 0
    w = [None] * 4
    for a in (0, 1):
        w[a] = jnp.where(half, v[a], pltpu.roll(v[a + 2], 64, 1))
        w[a + 2] = jnp.where(half, pltpu.roll(v[a], 64, 1), v[a + 2])
    z = [None] * 4
    for a in (0, 2):
        z[a] = jnp.where(even, w[a], pltpu.roll(w[a + 1], 32, 1))
        z[a + 1] = jnp.where(even, pltpu.roll(w[a], 96, 1), w[a + 1])
    return z


def spread_matrix(t_ref):
    lane = lax.broadcasted_iota(jnp.int32, (1, WIDE), 1)
    i, j = lane >> 5, lane & 31
    source = jnp.where((j < BS) & (i < BS), i * BS + j, -1)
    entry = lax.broadcasted_iota(jnp.int32, (NB, WIDE), 0)
    t_ref[...] = jnp.where(entry == source, 1.0, 0.0).astype(BF16)


def slot_pick(rows, cols, count):
    slot = lax.broadcasted_iota(jnp.int32, (1, SA), 1)
    code = jnp.where(slot < count, cols * RB + rows, -1)
    place = lax.broadcasted_iota(jnp.int32, (KB * RB, SA), 0)
    return jnp.where(place == code, 1.0, 0.0).astype(BF16)


def column_spread(cols):
    lane = lax.broadcasted_iota(jnp.int32, (BPK, 128), 1)
    none = jnp.zeros((BPK, 128), F32)
    spread = []
    for kap in range(KB):
        one = jnp.where(lane - 32 * (kap % 4) == cols[:, kap : kap + 1], 1.0, 0.0)
        spread.append(jnp.concatenate([one if g == kap // 4 else none for g in range(4)], axis=1))
    return jnp.concatenate(spread, axis=0).astype(BF16)


def left_panel(blocks, pick, t_ref, a_ref, base):
    wide = jnp.dot(blocks, t_ref[...], preferred_element_type=F32).astype(BF16)
    for q in range(QUADS):
        sums = jnp.dot(pick, wide[:, q * 128 : (q + 1) * 128], preferred_element_type=F32)
        for g in range(KB // 4):
            v = [sums[(4 * g + a) * RB : (4 * g + a + 1) * RB] for a in range(4)]
            for a, z in enumerate(swap_quads(v)):
                i = 4 * q + a
                if i < BS:
                    hi = z.astype(BF16)
                    lo = (z - hi.astype(F32)).astype(BF16)
                    at = base + g * 128
                    a_ref[i * RB : (i + 1) * RB, at : at + 128] = hi
                    a_ref[(BS + i) * RB : (BS + i + 1) * RB, at : at + 128] = lo


def right_panel(blocks, spread, w_ref, b_ref, base):
    w_ref[528:552, :] = jnp.zeros((24, 128), F32)
    w_ref[0:NB, :] = blocks.astype(F32)
    pad = jnp.zeros((8, 128), F32)
    for q in range(QUADS):
        entries = []
        for a in range(4):
            k = 4 * q + a
            if k < BS:
                entries += [w_ref[pl.ds(k, 24, stride=BS), :], pad]
            else:
                entries += [pad] * 4
        entries = jnp.concatenate(entries, axis=0).astype(BF16)
        full = jnp.dot(entries, spread, preferred_element_type=F32)
        for g in range(4):
            v = [full[a * JP : (a + 1) * JP, g * 128 : (g + 1) * 128] for a in range(4)]
            for a, z in enumerate(swap_quads(v)):
                at = base + (4 * g + a) * JP
                b_ref[at : at + JP, q * 128 : (q + 1) * 128] = z.astype(BF16)


def multiply(a_ref, b_ref, p_ref):
    for q in range(QUADS):
        both = jnp.dot(a_ref[...], b_ref[:, q * 128 : (q + 1) * 128], preferred_element_type=F32)
        for i in range(BS):
            total = both[i * RB : (i + 1) * RB] + both[(BS + i) * RB : (BS + i + 1) * RB]
            p_ref[q, pl.ds(i, RB, stride=24), :] = total


def first_kernel(counts_hbm, rows_hbm, cols_hbm, kcols_hbm, l_hbm, r_hbm,
                 p_ref, t_ref, pick_ref, spread_ref,
                 counts, rows, cols, kcols, l_ref, r_ref, a_ref, w_ref, b_ref, sems):
    moves = [
        pltpu.make_async_copy(s, d, sems.at[n])
        for n, (s, d) in enumerate((
            (counts_hbm, counts), (rows_hbm, rows), (cols_hbm, cols), (kcols_hbm, kcols),
            (l_hbm, l_ref), (r_hbm, r_ref),
        ))
    ]
    for move in moves:
        move.start()
    spread_matrix(t_ref)
    for move in moves:
        move.wait()
    ncol, nrow = rows.shape[1], kcols.shape[0]
    for s in range(3):
        panel = lax.rem(lax.axis_index("col") + s, ncol)
        source = lax.rem(lax.axis_index("row") + s, nrow)
        pick_ref[s] = slot_pick(rows[0, pl.ds(panel, 1), :], cols[0, pl.ds(panel, 1), :], counts[0, panel])
        spread_ref[s] = column_spread(kcols[source])
    left_panel(l_ref[...], pick_ref[0], t_ref, a_ref, 0)
    right_panel(r_ref[...], spread_ref[0], w_ref, b_ref, 0)
    multiply(a_ref, b_ref, p_ref)


def left_kernel(l1, l2, t_ref, pick_ref, a_ref):
    left_panel(l1[...], pick_ref[1], t_ref, a_ref, 0)
    left_panel(l2[...], pick_ref[2], t_ref, a_ref, DEPTH)


def last_kernel(a_ref, r1, r2, spread_ref, first_ref, out_hbm, w_ref, b_ref, p_ref, o_ref, sems):
    right_panel(r1[...], spread_ref[1], w_ref, b_ref, 0)
    right_panel(r2[...], spread_ref[2], w_ref, b_ref, DEPTH)
    multiply(a_ref, b_ref, p_ref)
    out = out_hbm.reshape(NB * 4, 128)
    moves = []
    for ib in range(3):
        n = 8 if ib < 2 else 7
        for rq in range(RB // 4):
            for q in range(QUADS):
                at = [(4 * rq + a) * 24 + ib * 8 for a in range(4)]
                v = [p_ref[q, t : t + 8, :] + first_ref[q, t : t + 8, :] for t in at]
                for a, z in enumerate(swap_quads(v)):
                    k = 4 * q + a
                    if k < BS:
                        o_ref[pl.ds((ib * 8 * BS + k) * 4 + rq, n, stride=4 * BS), :] = z[:n]
        part = pl.ds(ib * 8 * BS * 4, n * BS * 4)
        moves.append(pltpu.make_async_copy(o_ref.at[part], out.at[part], sems.at[ib]))
        moves[-1].start()
    for move in moves:
        move.wait()


VMEM = pl.BlockSpec(memory_space=pltpu.VMEM)
ANY = pl.BlockSpec(memory_space=pl.ANY)
LIMIT = pltpu.CompilerParams(vmem_limit_bytes=24 * 1024 * 1024)


def shape(*dims, dtype=F32):
    return jax.ShapeDtypeStruct(dims, dtype)


def body(left_blocks, left_rows, left_cols, left_counts, right_blocks, right_cols):
    left = left_blocks[0, 0]
    right = jnp.swapaxes(right_blocks[0, 0], 0, 1)
    kcols = jnp.swapaxes(right_cols[:, 0], 1, 2)
    l2, l1 = from_behind(left, "col", -2), from_behind(left, "col", -1)
    r2, r1 = from_behind(right, "row", -2), from_behind(right, "row", -1)
    first, spread_t, pick, spread = pl.pallas_call(
        first_kernel,
        out_shape=(shape(QUADS, RB * 24, 128), shape(NB, WIDE, dtype=BF16),
                   shape(3, KB * RB, SA, dtype=BF16), shape(3, KB * BPK, KB * CB, dtype=BF16)),
        in_specs=[ANY] * 6,
        out_specs=(VMEM,) * 4,
        scratch_shapes=[
            pltpu.SMEM(left_counts.shape, jnp.int32),
            pltpu.VMEM(left_rows.shape, jnp.int32),
            pltpu.VMEM(left_cols.shape, jnp.int32),
            pltpu.VMEM(kcols.shape, jnp.int32),
            pltpu.VMEM((SA, NB), BF16),
            pltpu.VMEM((NB, 128), BF16),
            pltpu.VMEM((2 * BS * RB, DEPTH), BF16),
            pltpu.VMEM((552, 128), F32),
            pltpu.VMEM((DEPTH, WIDE), BF16),
            pltpu.SemaphoreType.DMA((6,)),
        ],
        compiler_params=LIMIT,
        cost_estimate=pl.CostEstimate(flops=1, bytes_accessed=1, transcendentals=0),
    )(*(pltpu.with_memory_space_constraint(x, pltpu.HBM) for x in (left_counts, left_rows, left_cols, kcols, left, right)))
    dense = pl.pallas_call(
        left_kernel,
        out_shape=shape(2 * BS * RB, 2 * DEPTH, dtype=BF16),
        in_specs=[VMEM] * 4,
        out_specs=VMEM,
        compiler_params=LIMIT,
        cost_estimate=pl.CostEstimate(flops=10**10, bytes_accessed=4 * 10**6, transcendentals=0),
    )(l1, l2, spread_t, pick)
    out = pl.pallas_call(
        last_kernel,
        out_shape=shape(NB, 1, RB * CB),
        in_specs=[VMEM] * 5,
        out_specs=ANY,
        scratch_shapes=[
            pltpu.VMEM((552, 128), F32),
            pltpu.VMEM((2 * DEPTH, WIDE), BF16),
            pltpu.VMEM((QUADS, RB * 24, 128), F32),
            pltpu.VMEM((2120, 128), F32),
            pltpu.SemaphoreType.DMA((3,)),
        ],
        compiler_params=LIMIT,
        cost_estimate=pl.CostEstimate(flops=10**9, bytes_accessed=8 * 10**6, transcendentals=0),
    )(dense, r1, r2, spread, first)
    return jnp.transpose(out[None], (0, 2, 3, 1))


def solution(mesh):
    in_specs = (
        P("row", "col", None, None),
        P("row", None, None),
        P("row", None, None),
        P("row", None),
        P("row", "col", None, None),
        P(None, "col", None, None),
    )
    out_specs = P("row", "col", None, None)
    return jax.shard_map(body, mesh=mesh, in_specs=in_specs, out_specs=out_specs, check_vma=False)
```

time: 25.2 us -> 16.9 us (0.67)
  local copies, waits for them, and re-layouts: 6.45 us -> 0 us
  waiting for transfers between devices: 4.17 us -> 0.54 us
  Pallas kernels: 6.39 us -> 8.72 us
  starting transfers between devices: 7.83 us -> 7.5 us
    unnamed x12 -> x0, local copies, waits for them, and re-layouts: 4.56 us -> none
    ppermute x4, waiting for transfers between devices: 4.17 us -> 0.54 us  [from_behind(): lax.ppermute(value, axis, [(i, (i + by) % devices) for i in range(devices)])]
    pallas_call x1 -> x3, Pallas kernels: 6.39 us -> 8.72 us  [the longest x1 4.09 us: body(): pl.pallas_call(last_kernel, out_shape=shape(NB, 1, RB * CB), in_specs=[VM...]
    broadcast_in_dim x1 -> x0, local copies, waits for them, and re-layouts: 1.73 us -> none  [body(): return jnp.swapaxes(out.reshape(NB, RB * CB), 0, 1)[None, None]]
    ppermute x4, starting transfers between devices: 7.83 us -> 7.5 us  [from_behind(): lax.ppermute(value, axis, [(i, (i + by) % devices) for i in range(devices)])]
  transfers between devices with their start and end apart: 4 -> 4, of which waited for: 1 -> 2; matrix products, arithmetic and copies ran while one was open for 0% -> 0% of each run, Pallas kernels for 0% -> 28%
where the time goes in v2:
time: 16.9 us; the launch traced here: 16.8 us
  Pallas kernels  8.72 us (52%)
  starting transfers between devices  7.5 us (44%)
  waiting for transfers between devices  0.54 us (3%)
    ppermute x4, starting transfers between devices, from_behind(): lax.ppermute(value, axis, [(i, (i + by) % devices) for i in range(devices)])  7.5 us
    pallas_call x1, Pallas kernels, body(): pl.pallas_call(last_kernel, out_shape=shape(NB, 1, RB * CB), in_specs=[VM...  4.09 us
    pallas_call x1, Pallas kernels, body(): pl.pallas_call(first_kernel, out_shape=(shape(QUADS, RB * 24, 128), shape...  3.35 us
    pallas_call x1, Pallas kernels, body(): pl.pallas_call(left_kernel, out_shape=shape(2 * BS * RB, 2 * DEPTH, dtype...  1.28 us
    ppermute x4, waiting for transfers between devices, from_behind(): lax.ppermute(value, axis, [(i, (i + by) % devices) for i in range(devices)])  0.54 us
  transfers between devices with their start and end apart: 4, of which 2 were waited for; matrix products, arithmetic and copies ran while one was open for 0% of the time, Pallas kernels for 28%

profile of v2, /device:TPU:0, one launch (start us, length us, event | category | flops | bytes accessed | tf_op | source)
XLA Modules:
  0.0 16.8 jit_solution(2823116964411885343)
XLA Ops:
  0.0 5.0 %collective-permute-start = (bf16[64,529]{1,0:T(8,128)(2,1)}, bf16[64,529]{1,0:T(8,128)(2,1)S(1)}, u32[]{:S(2)}, u32[]{:S(2)}) collective-permute-start(bf16[64,529]{1,0:T(8,128)(2,1)} %bitcast.13), channel_id=1, source_target_pairs={{0,3},{1,0},{2,1},{3,2},{4,7},{5,4},{6,5},{7,6},{8,11},{9,8},{10,9... | collective-permute-start | bytes 203144 | tf_op jit(solution)/shard_map/ppermute | solution.py:26
  5.0 0.0 collective-permute-start.1
  5.1 1.6 %collective-permute-start.2 = (bf16[529,128]{1,0:T(8,128)(2,1)}, bf16[529,128]{1,0:T(8,128)(2,1)S(1)}, u32[]{:S(2)}, u32[]{:S(2)}) collective-permute-start(bf16[529,128]{1,0:T(8,128)(2,1)} %bitcast.10), channel_id=1, source_target_pairs={{0,28},{4,0},{8,4},{12,8},{16,12},{20,16},{24,20},{28,24},{1,29},{... | collective-permute-start | bytes 406280 | tf_op jit(solution)/shard_map/ppermute | solution.py:26
  6.7 0.8 %collective-permute-start.3 = (bf16[529,128]{1,0:T(8,128)(2,1)}, bf16[529,128]{1,0:T(8,128)(2,1)S(1)}, u32[]{:S(2)}, u32[]{:S(2)}) collective-permute-start(bf16[529,128]{1,0:T(8,128)(2,1)} %bitcast.11), channel_id=1, source_target_pairs={{0,24},{4,28},{8,0},{12,4},{16,8},{20,12},{24,16},{28,20},{1,25},{... | collective-permute-start | bytes 406280 | tf_op jit(solution)/shard_map/ppermute | solution.py:26
  7.5 3.3 %shard_map.64 = (f32[6,384,128]{2,1,0:T(8,128)S(1)}, bf16[529,768]{1,0:T(8,128)(2,1)S(1)}, bf16[3,256,64]{2,1,0:T(8,128)(2,1)S(1)}, bf16[3,128,512]{2,1,0:T(8,128)(2,1)S(1)}) custom-call(s32[1,4]{1,0:T(1,128)} %counts_hbm.1, s32[1,4,64]{2,1,0:T(4,128)} %rows_hbm.1, s32[1,4,64]{2,1,0:T(4,128)} %cols_hbm.1, s32[8,8,16]{2,1,0:T(8,128)} %bitcast.16, ...), custom_call_target="tpu_custom_call" | custom-call | flops 1 | bytes 1 | tf_op jit(solution)/shard_map/pallas_call | solution.py:183
  10.9 0.0 collective-permute-done.l1
  10.9 0.2 collective-permute-done.1.l2
  11.0 1.3 %shard_map.65.a_ref = bf16[736,1024]{1,0:T(8,128)(2,1)S(1)} custom-call(bf16[64,529]{1,0:T(8,128)(2,1)S(1)} %collective-permute-done.l1, bf16[64,529]{1,0:T(8,128)(2,1)S(1)} %collective-permute-done.1.l2, bf16[529,768]{1,0:T(8,128)(2,1)S(1)} %get-tuple-element.9.t_ref, bf16[3,256,64]{2,1,0:T(8,128)(2,1)S(1)} %get-tuple-element.10.pick_ref), custom_call_target="tpu_custom_call" | custom-call | flops 10000000000 | bytes 4000000 | tf_op jit(solution)/shard_map/pallas_call | solution.py:204
  12.3 0.0 collective-permute-done.2.r1
  12.3 0.4 %collective-permute-done.3.r2 = bf16[529,128]{1,0:T(8,128)(2,1)S(1)} collective-permute-done((bf16[529,128]{1,0:T(8,128)(2,1)}, bf16[529,128]{1,0:T(8,128)(2,1)S(1)}, u32[]{:S(2)}, u32[]{:S(2)}) %collective-permute-start.3) | collective-permute-done | bytes 135456 | tf_op jit(solution)/shard_map/ppermute | solution.py:26
  12.7 4.1 %shard_map.66 = f32[529,1,512]{2,1,0:T(1,128)} custom-call(bf16[736,1024]{1,0:T(8,128)(2,1)S(1)} %shard_map.65.a_ref, bf16[529,128]{1,0:T(8,128)(2,1)S(1)} %collective-permute-done.2.r1, bf16[529,128]{1,0:T(8,128)(2,1)S(1)} %collective-permute-done.3.r2, bf16[3,128,512]{2,1,0:T(8,128)(2,1)S(1)} %get-tuple-element.11.spread_ref, ...), custom_call_target="tpu_custom_call" | custom-call | flops 1000000000 | bytes 8000000 | tf_op jit(solution)/shard_map/pallas_call | solution.py:212
Async XLA Ops:
  0.0 10.9 %collective-permute-start = (bf16[64,529]{1,0:T(8,128)(2,1)}, bf16[64,529]{1,0:T(8,128)(2,1)S(1)}, u32[]{:S(2)}, u32[]{:S(2)}) collective-permute-start(bf16[64,529]{1,0:T(8,128)(2,1)} %bitcast.13), channel_id=1, source_target_pairs={{0,3},{1,0},{2,1},{3,2},{4,7},{5,4},{6,5},{7,6},{8,11},{9,8},{10,9... | collective-permute-start | bytes 203144 | tf_op jit(solution)/shard_map/ppermute | solution.py:26
  5.0 6.0 %collective-permute-start.1 = (bf16[64,529]{1,0:T(8,128)(2,1)}, bf16[64,529]{1,0:T(8,128)(2,1)S(1)}, u32[]{:S(2)}, u32[]{:S(2)}) collective-permute-start(bf16[64,529]{1,0:T(8,128)(2,1)} %bitcast.14), channel_id=1, source_target_pairs={{0,2},{1,3},{2,0},{3,1},{4,6},{5,7},{6,4},{7,5},{8,10},{9,11},{10,... | collective-permute-start | bytes 203144 | tf_op jit(solution)/shard_map/ppermute | solution.py:26
  5.1 7.3 %collective-permute-start.2 = (bf16[529,128]{1,0:T(8,128)(2,1)}, bf16[529,128]{1,0:T(8,128)(2,1)S(1)}, u32[]{:S(2)}, u32[]{:S(2)}) collective-permute-start(bf16[529,128]{1,0:T(8,128)(2,1)} %bitcast.10), channel_id=1, source_target_pairs={{0,28},{4,0},{8,4},{12,8},{16,12},{20,16},{24,20},{28,24},{1,29},{... | collective-permute-start | bytes 406280 | tf_op jit(solution)/shard_map/ppermute | solution.py:26
  6.7 6.0 %collective-permute-start.3 = (bf16[529,128]{1,0:T(8,128)(2,1)}, bf16[529,128]{1,0:T(8,128)(2,1)S(1)}, u32[]{:S(2)}, u32[]{:S(2)}) collective-permute-start(bf16[529,128]{1,0:T(8,128)(2,1)} %bitcast.11), channel_id=1, source_target_pairs={{0,24},{4,28},{8,0},{12,4},{16,8},{20,12},{24,16},{28,20},{1,25},{... | collective-permute-start | bytes 406280 | tf_op jit(solution)/shard_map/ppermute | solution.py:26

commit v3 on v2

v3 whole, which is shorter than its diff:
```python
import jax
import jax.numpy as jnp
from jax import lax
from jax.experimental import pallas as pl
from jax.experimental.pallas import tpu as pltpu
from jax.sharding import PartitionSpec as P

BS = 23
RB = 16
CB = 32
KB = 16
BPK = 8
SA = 64
JP = 32
QUADS = 6
NB = BS * BS
ROWS = BS * RB
WIDE = QUADS * 128
DEPTH = KB * JP
BANDS = ((0, 256), (128, 384), (256, NB))
F32 = jnp.float32
BF16 = jnp.bfloat16


def from_behind(value, axis, by):
    devices = lax.axis_size(axis)
    return lax.ppermute(value, axis, [(i, (i + by) % devices) for i in range(devices)])


def lanes_like(v):
    return lax.broadcasted_iota(jnp.int32, v.shape, 1)


def unrotate(v, shift):
    chunk = lanes_like(v[0]) >> 5
    z = v[(3 - shift) % 4]
    for p in range(3):
        z = jnp.where(chunk == p, v[(p - shift) % 4], z)
    return pltpu.roll(z, 128 - 32 * shift, 1) if shift else z


def spread_matrix(t_ref):
    for u, (start, stop) in enumerate(BANDS):
        lane = lax.broadcasted_iota(jnp.int32, (1, 256), 1) + 256 * u
        i, j = lane >> 5, lane & 31
        source = jnp.where((j < BS) & (i < BS), i * BS + j, -1)
        entry = lax.broadcasted_iota(jnp.int32, (stop - start, 256), 0) + start
        t_ref[start:stop, 256 * u : 256 * (u + 1)] = jnp.where(entry == source, 1.0, 0.0).astype(BF16)


def slot_pick(rows, cols, count):
    slot = lax.broadcasted_iota(jnp.int32, (1, SA), 1)
    code = (cols & 3) * 64 + (cols >> 2) * RB + rows
    code = jnp.where(slot < count, code, -1)
    place = lax.broadcasted_iota(jnp.int32, (KB * RB, SA), 0)
    return jnp.where(place == code, 1.0, 0.0).astype(BF16)


def column_spread(cols, turn):
    lane = lax.broadcasted_iota(jnp.int32, (BPK, 128), 1)
    none = jnp.zeros((BPK, 128), F32)
    spread = []
    for kap in range(KB):
        one = jnp.where(lane - 32 * ((kap + turn) % 4) == cols[:, kap : kap + 1], 1.0, 0.0)
        spread.append(jnp.concatenate([one if g == kap // 4 else none for g in range(4)], axis=1))
    return jnp.concatenate(spread, axis=0).astype(BF16)


def left_panel(l_ref, pick, t_ref, a_ref):
    for u, (start, stop) in enumerate(BANDS):
        wide = jnp.dot(l_ref[:, start:stop], t_ref[start:stop, 256 * u : 256 * (u + 1)], preferred_element_type=F32)
        sums = []
        for a in range(4):
            turned = wide
            if a:
                turned = jnp.concatenate([pltpu.roll(wide[:, h : h + 128], 32 * a, 1) for h in (0, 128)], axis=1)
            sums.append(jnp.dot(pick[64 * a : 64 * (a + 1)], turned.astype(BF16), preferred_element_type=F32))
        for h in range(2):
            for g in range(KB // 4):
                v = [s[g * RB : (g + 1) * RB, h * 128 : (h + 1) * 128] for s in sums]
                for a in range(4):
                    i = 8 * u + 4 * h + a
                    if i < BS:
                        z = unrotate(v, a)
                        hi = z.astype(BF16)
                        lo = (z - hi.astype(F32)).astype(BF16)
                        a_ref[i * RB : (i + 1) * RB, g * 128 : (g + 1) * 128] = hi
                        a_ref[(BS + i) * RB : (BS + i + 1) * RB, g * 128 : (g + 1) * 128] = lo


def right_panel(r_ref, spread_ref, w_ref, b_ref):
    w_ref[528:552, :] = jnp.zeros((24, 128), F32)
    w_ref[0:NB, :] = r_ref[...].astype(F32)
    pad = jnp.zeros((8, 128), F32)
    full = []
    for a in range(4):
        entries = []
        for q in range(QUADS):
            k = 4 * q + a
            if k < BS:
                entries += [w_ref[pl.ds(k, 24, stride=BS), :], pad]
            else:
                entries += [pad] * 4
        entries = jnp.concatenate(entries, axis=0).astype(BF16)
        full.append(jnp.dot(entries, spread_ref[a], preferred_element_type=F32))
    for q in range(QUADS):
        for g in range(4):
            v = [f[q * JP : q * JP + 24, g * 128 : (g + 1) * 128] for f in full]
            for a in range(4):
                z = jnp.concatenate([unrotate(v, a), pad], axis=0).astype(BF16)
                at = (4 * g + a) * JP
                b_ref[at : at + JP, q * 128 : (q + 1) * 128] = z


def multiply(a_ref, b_ref, p_ref, add_ref=None):
    for u in range(3):
        both = jnp.dot(a_ref[...], b_ref[:, 256 * u : 256 * (u + 1)], preferred_element_type=F32)
        for i in range(BS):
            total = both[i * RB : (i + 1) * RB] + both[(BS + i) * RB : (BS + i + 1) * RB]
            for h in range(2):
                part = total[:, 128 * h : 128 * (h + 1)]
                at = (2 * u + h, pl.ds(i, RB, stride=24), slice(None))
                p_ref[at] = part if add_ref is None else part + add_ref[at]


def first_kernel(counts_hbm, rows_hbm, cols_hbm, kcols_hbm, l_hbm, r_hbm,
                 p_ref, t_ref, pick_ref, spread_ref,
                 counts, rows, cols, kcols, l_ref, r_ref, a_ref, w_ref, b_ref, sems):
    moves = [
        pltpu.make_async_copy(s, d, sems.at[n])
        for n, (s, d) in enumerate((
            (counts_hbm, counts), (rows_hbm, rows), (cols_hbm, cols), (kcols_hbm, kcols),
            (l_hbm, l_ref), (r_hbm, r_ref),
        ))
    ]
    for move in moves:
        move.start()
    spread_matrix(t_ref)
    for move in moves:
        move.wait()
    ncol, nrow = rows.shape[1], kcols.shape[0]
    for s in range(3):
        panel = lax.rem(lax.axis_index("col") + s, ncol)
        source = lax.rem(lax.axis_index("row") + s, nrow)
        pick_ref[s] = slot_pick(rows[0, pl.ds(panel, 1), :], cols[0, pl.ds(panel, 1), :], counts[0, panel])
        for a in range(4):
            spread_ref[s, a] = column_spread(kcols[source], a)
    left_panel(l_ref, pick_ref[0], t_ref, a_ref)
    right_panel(r_ref, spread_ref.at[0], w_ref, b_ref)
    multiply(a_ref, b_ref, p_ref)


def far_left_kernel(l2, t_ref, pick_ref, _, a_ref):
    left_panel(l2, pick_ref[2], t_ref, a_ref)


def far_right_kernel(a_ref, r2, spread_ref, first_ref, p_ref, w_ref, b_ref):
    right_panel(r2, spread_ref.at[2], w_ref, b_ref)
    multiply(a_ref, b_ref, p_ref, first_ref)


def near_right_kernel(r1, spread_ref, _, b_ref, w_ref):
    right_panel(r1, spread_ref.at[1], w_ref, b_ref)


def last_kernel(l1, t_ref, pick_ref, b_ref, before_ref, out_hbm, a_ref, p_ref, h_ref, o_ref, sems):
    left_panel(l1, pick_ref[1], t_ref, a_ref)
    multiply(a_ref, b_ref, p_ref)
    out = out_hbm.reshape(NB * 4, 128)
    moves = []
    for ib in range(3):
        n = 8 if ib < 2 else 7
        for rq in range(RB // 4):
            for q in range(QUADS):
                at = [(4 * rq + a) * 24 + ib * 8 for a in range(4)]
                v = [p_ref[q, t : t + 8, :] + before_ref[q, t : t + 8, :] for t in at]
                half = lanes_like(v[0]) < 64
                for a in (0, 1):
                    h_ref[q, rq, a] = jnp.where(half, v[a], pltpu.roll(v[a + 2], 64, 1))
                    h_ref[q, rq, a + 2] = jnp.where(half, pltpu.roll(v[a], 64, 1), v[a + 2])
        for rq in range(RB // 4):
            for q in range(QUADS):
                for a in (0, 2):
                    x, y = h_ref[q, rq, a], h_ref[q, rq, a + 1]
                    even = (lanes_like(x) & 32) == 0
                    z = (jnp.where(even, x, pltpu.roll(y, 32, 1)), jnp.where(even, pltpu.roll(x, 96, 1), y))
                    for b in range(2):
                        k = 4 * q + a + b
                        if k < BS:
                            o_ref[pl.ds((ib * 8 * BS + k) * 4 + rq, n, stride=4 * BS), :] = z[b][:n]
        part = pl.ds(ib * 8 * BS * 4, n * BS * 4)
        moves.append(pltpu.make_async_copy(o_ref.at[part], out.at[part], sems.at[ib]))
        moves[-1].start()
    for move in moves:
        move.wait()


VMEM = pl.BlockSpec(memory_space=pltpu.VMEM)
ANY = pl.BlockSpec(memory_space=pl.ANY)


def shape(*dims, dtype=F32):
    return jax.ShapeDtypeStruct(dims, dtype)


def call(kernel, flops, out_shape, in_specs, out_specs, scratch):
    return pl.pallas_call(
        kernel,
        out_shape=out_shape,
        in_specs=in_specs,
        out_specs=out_specs,
        scratch_shapes=scratch,
        compiler_params=pltpu.CompilerParams(vmem_limit_bytes=24 * 1024 * 1024),
        cost_estimate=pl.CostEstimate(flops=flops, bytes_accessed=1, transcendentals=0),
    )


def body(left_blocks, left_rows, left_cols, left_counts, right_blocks, right_cols):
    left = left_blocks[0, 0]
    right = jnp.swapaxes(right_blocks[0, 0], 0, 1)
    kcols = jnp.swapaxes(right_cols[:, 0], 1, 2)
    l2, r2 = from_behind(left, "col", -2), from_behind(right, "row", -2)
    r1, l1 = from_behind(right, "row", -1), from_behind(left, "col", -1)
    sums = shape(QUADS, RB * 24, 128)
    dense_left = shape(2 * ROWS, DEPTH, dtype=BF16)
    dense_right = shape(DEPTH, WIDE, dtype=BF16)
    a_scratch = pltpu.VMEM(dense_left.shape, BF16)
    b_scratch = pltpu.VMEM(dense_right.shape, BF16)
    w_scratch = pltpu.VMEM((552, 128), F32)
    first, spread_t, pick, spread = call(
        first_kernel, 1,
        (sums, shape(NB, WIDE, dtype=BF16), shape(3, KB * RB, SA, dtype=BF16), shape(3, 4, KB * BPK, KB * CB, dtype=BF16)),
        [ANY] * 6, (VMEM,) * 4,
        [
            pltpu.SMEM(left_counts.shape, jnp.int32),
            pltpu.VMEM(left_rows.shape, jnp.int32),
            pltpu.VMEM(left_cols.shape, jnp.int32),
            pltpu.VMEM(kcols.shape, jnp.int32),
            pltpu.VMEM((SA, NB), BF16),
            pltpu.VMEM((NB, 128), BF16),
            a_scratch, w_scratch, b_scratch,
            pltpu.SemaphoreType.DMA((6,)),
        ],
    )(*(pltpu.with_memory_space_constraint(x, pltpu.HBM) for x in (left_counts, left_rows, left_cols, kcols, left, right)))
    far_left = call(far_left_kernel, 10**10, dense_left, [VMEM] * 3 + [ANY], VMEM, [])(l2, spread_t, pick, first)
    before = call(
        far_right_kernel, 10**10, sums, [VMEM] * 4, VMEM, [w_scratch, b_scratch],
    )(far_left, r2, spread, first)
    near_right = call(near_right_kernel, 10**10, dense_right, [VMEM] * 2 + [ANY], VMEM, [w_scratch])(r1, spread, before)
    out = call(
        last_kernel, 10**10, shape(NB, 1, RB * CB), [VMEM] * 5, ANY,
        [
            a_scratch,
            pltpu.VMEM(sums.shape, F32),
            pltpu.VMEM((QUADS, 4, 4, 8, 128), F32),
            pltpu.VMEM((2120, 128), F32),
            pltpu.SemaphoreType.DMA((3,)),
        ],
    )(l1, spread_t, pick, near_right, before)
    return jnp.transpose(out[None], (0, 2, 3, 1))


def solution(mesh):
    in_specs = (
        P("row", "col", None, None),
        P("row", None, None),
        P("row", None, None),
        P("row", None),
        P("row", "col", None, None),
        P(None, "col", None, None),
    )
    out_specs = P("row", "col", None, None)
    return jax.shard_map(body, mesh=mesh, in_specs=in_specs, out_specs=out_specs, check_vma=False)
```

time: 16.9 us -> 17.4 us (1.030)
  Pallas kernels: 8.72 us -> 9.36 us
  waiting for transfers between devices: 0.54 us -> 0.01 us
  starting transfers between devices: 7.5 us -> 7.83 us
    pallas_call x3 -> x5, Pallas kernels: 8.72 us -> 9.36 us  [the longest x1 3.25 us: body(): call(last_kernel, 10 ** 10, shape(NB, 1, RB * CB), [VMEM] * 5, ANY, [a_sc...]
    ppermute x4, waiting for transfers between devices: 0.54 us -> 0.01 us  [from_behind(): lax.ppermute(value, axis, [(i, (i + by) % devices) for i in range(devices)])]
    ppermute x4, starting transfers between devices: 7.5 us -> 7.83 us  [from_behind(): lax.ppermute(value, axis, [(i, (i + by) % devices) for i in range(devices)])]
  transfers between devices with their start and end apart: 4 -> 4, of which waited for: 2 -> 0; matrix products, arithmetic and copies ran while one was open for 0% -> 0% of each run, Pallas kernels for 28% -> 35%
where the time goes in v3:
time: 17.4 us; the launch traced here: 17.3 us
  Pallas kernels  9.36 us (54%)
  starting transfers between devices  7.83 us (45%)
    ppermute x4, starting transfers between devices, from_behind(): lax.ppermute(value, axis, [(i, (i + by) % devices) for i in range(devices)])  7.83 us
    pallas_call x1, Pallas kernels, body(): call(last_kernel, 10 ** 10, shape(NB, 1, RB * CB), [VMEM] * 5, ANY, [a_sc...  3.25 us
    pallas_call x1, Pallas kernels, body(): call(first_kernel, 1, (sums, shape(NB, WIDE, dtype=BF16), shape(3, KB * R...  3.15 us
    pallas_call x1, Pallas kernels, body(): call(far_right_kernel, 10 ** 10, sums, [VMEM] * 4, VMEM, [w_scratch, b_sc...  1.38 us
    pallas_call x1, Pallas kernels, body(): call(far_left_kernel, 10 ** 10, dense_left, [VMEM] * 3 + [ANY], VMEM, [])  1.03 us
    pallas_call x1, Pallas kernels, body(): call(near_right_kernel, 10 ** 10, dense_right, [VMEM] * 2 + [ANY], VMEM,...  0.56 us
  transfers between devices with their start and end apart: 4, of which 0 were waited for; matrix products, arithmetic and copies ran while one was open for 0% of the time, Pallas kernels for 35%

profile of v3, /device:TPU:0, one launch (start us, length us, event | category | flops | bytes accessed | tf_op | source)
XLA Modules:
  0.0 17.3 jit_solution(11509705389838569168)
XLA Ops:
  0.0 4.0 %collective-permute-start.2 = (bf16[64,529]{1,0:T(8,128)(2,1)}, bf16[64,529]{1,0:T(8,128)(2,1)S(1)}, u32[]{:S(2)}, u32[]{:S(2)}) collective-permute-start(bf16[64,529]{1,0:T(8,128)(2,1)} %bitcast.13), channel_id=1, source_target_pairs={{0,2},{1,3},{2,0},{3,1},{4,6},{5,7},{6,4},{7,5},{8,10},{9,11},{10,... | collective-permute-start | bytes 203144 | tf_op jit(solution)/shard_map/ppermute | solution.py:27
  4.0 2.4 %collective-permute-start.3 = (bf16[529,128]{1,0:T(8,128)(2,1)}, bf16[529,128]{1,0:T(8,128)(2,1)S(1)}, u32[]{:S(2)}, u32[]{:S(2)}) collective-permute-start(bf16[529,128]{1,0:T(8,128)(2,1)} %bitcast.10), channel_id=1, source_target_pairs={{0,24},{4,28},{8,0},{12,4},{16,8},{20,12},{24,16},{28,20},{1,25},{... | collective-permute-start | bytes 406280 | tf_op jit(solution)/shard_map/ppermute | solution.py:27
  6.5 0.0 collective-permute-start.1
  6.5 1.3 %collective-permute-start = (bf16[64,529]{1,0:T(8,128)(2,1)}, bf16[64,529]{1,0:T(8,128)(2,1)S(1)}, u32[]{:S(2)}, u32[]{:S(2)}) collective-permute-start(bf16[64,529]{1,0:T(8,128)(2,1)} %bitcast.14), channel_id=1, source_target_pairs={{0,3},{1,0},{2,1},{3,2},{4,7},{5,4},{6,5},{7,6},{8,11},{9,8},{10,9... | collective-permute-start | bytes 203144 | tf_op jit(solution)/shard_map/ppermute | solution.py:27
  7.8 3.1 %shard_map.64 = (f32[6,384,128]{2,1,0:T(8,128)S(1)}, bf16[529,768]{1,0:T(8,128)(2,1)S(1)}, bf16[3,256,64]{2,1,0:T(8,128)(2,1)S(1)}, bf16[3,4,128,512]{3,2,1,0:T(8,128)(2,1)S(1)}) custom-call(s32[1,4]{1,0:T(1,128)} %counts_hbm.1, s32[1,4,64]{2,1,0:T(4,128)} %rows_hbm.1, s32[1,4,64]{2,1,0:T(4,128)} %cols_hbm.1, s32[8,8,16]{2,1,0:T(8,128)} %bitcast.16, ...), custom_call_target="tpu_custom_call" | custom-call | flops 1 | bytes 1 | tf_op jit(solution)/shard_map/pallas_call | solution.py:230
  11.0 0.0 collective-permute-done.2.l2
  11.0 1.0 %shard_map.65.a_ref = bf16[736,512]{1,0:T(8,128)(2,1)S(1)} custom-call(bf16[64,529]{1,0:T(8,128)(2,1)S(1)} %collective-permute-done.2.l2, bf16[529,768]{1,0:T(8,128)(2,1)S(1)} %get-tuple-element.9.t_ref, bf16[3,256,64]{2,1,0:T(8,128)(2,1)S(1)} %get-tuple-element.10.pick_ref, f32[6,384,128]{2,1,0:T(8,128)S(1)} %get-tuple-element.12._.first_ref), custom_call_target="tpu_custom_call" | custom-call | flops 10000000000 | bytes 1 | tf_op jit(solution)/shard_map/pallas_call | solution.py:245
  12.0 0.0 collective-permute-done.3.r2
  12.0 1.4 %shard_map.66._.before_ref = f32[6,384,128]{2,1,0:T(8,128)S(1)} custom-call(bf16[736,512]{1,0:T(8,128)(2,1)S(1)} %shard_map.65.a_ref, bf16[529,128]{1,0:T(8,128)(2,1)S(1)} %collective-permute-done.3.r2, bf16[3,4,128,512]{3,2,1,0:T(8,128)(2,1)S(1)} %get-tuple-element.11.spread_ref, f32[6,384,128]{2,1,0:T(8,128)S(1)} %get-tuple-element.12._.first_ref), custom_call_target="tpu_custom_call" | custom-call | flops 10000000000 | bytes 1 | tf_op jit(solution)/shard_map/pallas_call | solution.py:246
  13.4 0.0 collective-permute-done.1.r1
  13.4 0.6 %shard_map.67.b_ref = bf16[512,768]{1,0:T(8,128)(2,1)S(1)} custom-call(bf16[529,128]{1,0:T(8,128)(2,1)S(1)} %collective-permute-done.1.r1, bf16[3,4,128,512]{3,2,1,0:T(8,128)(2,1)S(1)} %get-tuple-element.11.spread_ref, f32[6,384,128]{2,1,0:T(8,128)S(1)} %shard_map.66._.before_ref), custom_call_target="tpu_custom_call" | custom-call | flops 10000000000 | bytes 1 | tf_op jit(solution)/shard_map/pallas_call | solution.py:249
  14.0 0.0 collective-permute-done.l1
  14.0 3.2 %shard_map.68 = f32[529,1,512]{2,1,0:T(1,128)} custom-call(bf16[64,529]{1,0:T(8,128)(2,1)S(1)} %collective-permute-done.l1, bf16[529,768]{1,0:T(8,128)(2,1)S(1)} %get-tuple-element.9.t_ref, bf16[3,256,64]{2,1,0:T(8,128)(2,1)S(1)} %get-tuple-element.10.pick_ref, bf16[512,768]{1,0:T(8,128)(2,1)S(1)} %shard_map.67.b_ref, f32[6,384,128]{2,1,0:T(8,128)S(1)} %shard_map.66._.before_ref), custom_call_target="tpu_custom_call" | custom-call | flops 10000000000 | bytes 1 | tf_op jit(solution)/shard_map/pallas_call | solution.py:250
Async XLA Ops:
  0.0 11.0 %collective-permute-start.2 = (bf16[64,529]{1,0:T(8,128)(2,1)}, bf16[64,529]{1,0:T(8,128)(2,1)S(1)}, u32[]{:S(2)}, u32[]{:S(2)}) collective-permute-start(bf16[64,529]{1,0:T(8,128)(2,1)} %bitcast.13), channel_id=1, source_target_pairs={{0,2},{1,3},{2,0},{3,1},{4,6},{5,7},{6,4},{7,5},{8,10},{9,11},{10,... | collective-permute-start | bytes 203144 | tf_op jit(solution)/shard_map/ppermute | solution.py:27
  4.0 8.0 %collective-permute-start.3 = (bf16[529,128]{1,0:T(8,128)(2,1)}, bf16[529,128]{1,0:T(8,128)(2,1)S(1)}, u32[]{:S(2)}, u32[]{:S(2)}) collective-permute-start(bf16[529,128]{1,0:T(8,128)(2,1)} %bitcast.10), channel_id=1, source_target_pairs={{0,24},{4,28},{8,0},{12,4},{16,8},{20,12},{24,16},{28,20},{1,25},{... | collective-permute-start | bytes 406280 | tf_op jit(solution)/shard_map/ppermute | solution.py:27
  6.5 7.0 %collective-permute-start.1 = (bf16[529,128]{1,0:T(8,128)(2,1)}, bf16[529,128]{1,0:T(8,128)(2,1)S(1)}, u32[]{:S(2)}, u32[]{:S(2)}) collective-permute-start(bf16[529,128]{1,0:T(8,128)(2,1)} %bitcast.11), channel_id=1, source_target_pairs={{0,28},{4,0},{8,4},{12,8},{16,12},{20,16},{24,20},{28,24},{1,29},{... | collective-permute-start | bytes 406280 | tf_op jit(solution)/shard_map/ppermute | solution.py:27
  6.5 7.5 %collective-permute-start = (bf16[64,529]{1,0:T(8,128)(2,1)}, bf16[64,529]{1,0:T(8,128)(2,1)S(1)}, u32[]{:S(2)}, u32[]{:S(2)}) collective-permute-start(bf16[64,529]{1,0:T(8,128)(2,1)} %bitcast.14), channel_id=1, source_target_pairs={{0,3},{1,0},{2,1},{3,2},{4,7},{5,4},{6,5},{7,6},{8,11},{9,8},{10,9... | collective-permute-start | bytes 203144 | tf_op jit(solution)/shard_map/ppermute | solution.py:27

commit v4 on v3

v4 whole, which is shorter than its diff:
```python
import jax
import jax.numpy as jnp
from jax import lax
from jax.experimental import pallas as pl
from jax.experimental.pallas import tpu as pltpu
from jax.sharding import PartitionSpec as P

BS = 23
RB = 16
CB = 32
KB = 16
BPK = 8
SA = 64
JP = 32
QUADS = 6
NB = BS * BS
ROWS = BS * RB
WIDE = QUADS * 128
DEPTH = KB * JP
PAIRS = 12
SPANS = tuple((46 * u // 128 * 128, min(-(-min(46 * u + 46, NB) // 128) * 128, NB)) for u in range(PAIRS))
SPANS = tuple((start, NB if stop > 512 else stop) for start, stop in SPANS)
AT = tuple(sum(stop - start for start, stop in SPANS[:u]) for u in range(PAIRS + 1))
F32 = jnp.float32
BF16 = jnp.bfloat16


def from_behind(value, axis, by):
    devices = lax.axis_size(axis)
    return lax.ppermute(value, axis, [(i, (i + by) % devices) for i in range(devices)])


def lanes_like(v):
    return lax.broadcasted_iota(jnp.int32, v.shape, 1)


def unrotate(v, shift):
    chunk = lanes_like(v[0]) >> 5
    z = v[(3 - shift) % 4]
    for p in range(3):
        z = jnp.where(chunk == p, v[(p - shift) % 4], z)
    return pltpu.roll(z, 128 - 32 * shift, 1) if shift else z


def spread_matrix(t_ref):
    for u, (start, stop) in enumerate(SPANS):
        lane = lax.broadcasted_iota(jnp.int32, (1, 256), 1)
        i, j = 2 * u + (lane >> 7), lane & 31
        source = jnp.where((j < BS) & (i < BS), i * BS + j, -1)
        entry = lax.broadcasted_iota(jnp.int32, (stop - start, 256), 0) + start
        t_ref[AT[u] : AT[u + 1], :] = jnp.where(entry == source, 1.0, 0.0).astype(BF16)


def slot_pick(rows, cols, count):
    slot = lax.broadcasted_iota(jnp.int32, (1, SA), 1)
    code = jnp.where(slot < count, (cols >> 2) * RB + rows, -1)
    place = lax.broadcasted_iota(jnp.int32, (4 * RB, SA), 0)
    return jnp.where(place == code, 1.0, 0.0).astype(BF16)


def slot_mask(cols):
    quarter = lax.broadcasted_iota(jnp.int32, (8, SA), 0)
    mine = jnp.where(quarter == (cols & 3), 1.0, 0.0)
    lane = lax.broadcasted_iota(jnp.int32, (8, 256), 1)
    quarter = lax.broadcasted_iota(jnp.int32, (8, 256), 0)
    chunk = jnp.where(quarter == ((lane >> 5) & 3), 1.0, 0.0)
    return lax.dot_general(mine, chunk, (((0,), (0,)), ((), ())), preferred_element_type=F32).astype(BF16)


def column_spread(cols, spread_ref):
    lane = lax.broadcasted_iota(jnp.int32, (BPK, 128), 1)
    none = jnp.zeros((BPK, 128), F32)
    hits = [(lane & 31) == cols[:, kap : kap + 1] for kap in range(KB)]
    for turn in range(4):
        spread = []
        for kap in range(KB):
            one = jnp.where(hits[kap] & ((lane >> 5) == (kap + turn) % 4), 1.0, 0.0)
            spread.append(jnp.concatenate([one if g == kap // 4 else none for g in range(4)], axis=1))
        spread_ref[turn] = jnp.concatenate(spread, axis=0).astype(BF16)


def left_panel(l_ref, pick, mask, t_ref, a_ref):
    wide = []
    for u, (start, stop) in enumerate(SPANS):
        copies = jnp.dot(l_ref[:, start:stop], t_ref[AT[u] : AT[u + 1], :], preferred_element_type=F32)
        wide.append(copies.astype(BF16) * mask)
    for u in range(PAIRS):
        sums = jnp.dot(pick, wide[u], preferred_element_type=F32)
        hi = sums.astype(BF16)
        lo = (sums - hi.astype(F32)).astype(BF16)
        for h in range(2):
            i = 2 * u + h
            if i < BS:
                for g in range(KB // 4):
                    rows, lanes = slice(g * RB, (g + 1) * RB), slice(h * 128, (h + 1) * 128)
                    a_ref[i * RB : (i + 1) * RB, g * 128 : (g + 1) * 128] = hi[rows, lanes]
                    a_ref[(BS + i) * RB : (BS + i + 1) * RB, g * 128 : (g + 1) * 128] = lo[rows, lanes]


def right_panel(r_ref, spread_ref, w_ref, b_ref):
    w_ref[528:552, :] = jnp.zeros((24, 128), F32)
    w_ref[0:NB, :] = r_ref[...].astype(F32)
    pad = jnp.zeros((8, 128), F32)
    full = []
    for a in range(4):
        entries = []
        for q in range(QUADS):
            k = 4 * q + a
            if k < BS:
                entries += [w_ref[pl.ds(k, 24, stride=BS), :], pad]
            else:
                entries += [pad] * 4
        entries = jnp.concatenate(entries, axis=0).astype(BF16)
        full.append(jnp.dot(entries, spread_ref[a], preferred_element_type=F32))
    for q in range(QUADS):
        for g in range(4):
            v = [f[q * JP : q * JP + 24, g * 128 : (g + 1) * 128] for f in full]
            for a in range(4):
                z = jnp.concatenate([unrotate(v, a), pad], axis=0).astype(BF16)
                at = (4 * g + a) * JP
                b_ref[at : at + JP, q * 128 : (q + 1) * 128] = z


def product(panels, u):
    both = sum(jnp.dot(a[...], b[:, 256 * u : 256 * (u + 1)], preferred_element_type=F32) for a, b in panels)
    return both[:ROWS] + both[ROWS:]


def put_rows(p_ref, add_ref, total, u):
    for i in range(BS):
        for h in range(2):
            part = total[i * RB : (i + 1) * RB, 128 * h : 128 * (h + 1)]
            at = (2 * u + h, pl.ds(i, RB, stride=24), slice(None))
            p_ref[at] = part if add_ref is None else part + add_ref[at]


def first_kernel(counts_hbm, rows_hbm, cols_hbm, kcols_hbm, l_hbm, r_hbm,
                 a_ref, b_ref, r_ref, t_ref, pick_ref, mask_ref, spread_ref,
                 counts, rows, cols, kcols, l_ref, w_ref, sems):
    moves = [
        pltpu.make_async_copy(s, d, sems.at[n])
        for n, (s, d) in enumerate((
            (counts_hbm, counts), (rows_hbm, rows), (cols_hbm, cols), (kcols_hbm, kcols),
            (r_hbm, r_ref), (l_hbm, l_ref),
        ))
    ]
    for move in moves:
        move.start()
    spread_matrix(t_ref)
    for move in moves:
        move.wait()
    ncol, nrow = rows.shape[1], kcols.shape[0]
    for s in range(3):
        panel = lax.rem(lax.axis_index("col") + s, ncol)
        source = lax.rem(lax.axis_index("row") + s, nrow)
        panel_cols = cols[0, pl.ds(panel, 1), :]
        pick_ref[s] = slot_pick(rows[0, pl.ds(panel, 1), :], panel_cols, counts[0, panel])
        mask_ref[s] = slot_mask(panel_cols)
        column_spread(kcols[source], spread_ref.at[s])
    right_panel(r_ref, spread_ref.at[0], w_ref, b_ref)
    left_panel(l_ref, pick_ref[0], mask_ref[0], t_ref, a_ref)


def relay_kernel(r0, r2, _, x_ref):
    odd = lax.rem(lax.axis_index("row"), 2)

    @pl.when(odd == 1)
    def _():
        x_ref[...] = r0[...]

    @pl.when(odd == 0)
    def _():
        x_ref[...] = r2[...]


def far_right_kernel(r, spread_ref, a0, b0, _, b_ref, p_ref, w_ref):
    right_panel(r, spread_ref.at[2], w_ref, b_ref)
    for u in range(3):
        put_rows(p_ref, None, product(((a0, b0),), u), u)


def last_kernel(l2, l1, r1, t_ref, pick_ref, mask_ref, spread_ref, b2, before_ref, out_hbm, a2, a1, b1, w_ref, p_ref, h_ref, o_ref, sems):
    left_panel(l2, pick_ref[2], mask_ref[2], t_ref, a2)
    left_panel(l1, pick_ref[1], mask_ref[1], t_ref, a1)
    right_panel(r1, spread_ref.at[1], w_ref, b1)
    out = out_hbm.reshape(NB * 4, 128)
    moves = []
    for u in range(3):
        put_rows(p_ref, before_ref, product(((a2, b2), (a1, b1)), u), u)
        for part in ((0, 1, 2),) if u < 2 else ((0,), (1,), (2,)):
            places = [(q, rq, ib) for ib in part for q in (2 * u, 2 * u + 1) for rq in range(RB // 4)]
            for q, rq, ib in places:
                at = [(4 * rq + a) * 24 + ib * 8 for a in range(4)]
                v = [p_ref[q, t : t + 8, :] for t in at]
                half = lanes_like(v[0]) < 64
                for a in (0, 1):
                    h_ref[ib, q, rq, a] = jnp.where(half, v[a], pltpu.roll(v[a + 2], 64, 1))
                    h_ref[ib, q, rq, a + 2] = jnp.where(half, pltpu.roll(v[a], 64, 1), v[a + 2])
            for q, rq, ib in places:
                n = 8 if ib < 2 else 7
                for a in (0, 2):
                    x, y = h_ref[ib, q, rq, a], h_ref[ib, q, rq, a + 1]
                    even = (lanes_like(x) & 32) == 0
                    z = (jnp.where(even, x, pltpu.roll(y, 32, 1)), jnp.where(even, pltpu.roll(x, 96, 1), y))
                    for b in range(2):
                        k = 4 * q + a + b
                        if k < BS:
                            o_ref[pl.ds((ib * 8 * BS + k) * 4 + rq, n, stride=4 * BS), :] = z[b][:n]
            if u == 2:
                rows = pl.ds(part[0] * 8 * BS * 4, (8 if part[0] < 2 else 7) * BS * 4)
                moves.append(pltpu.make_async_copy(o_ref.at[rows], out.at[rows], sems.at[part[0]]))
                moves[-1].start()
    for move in moves:
        move.wait()


VMEM = pl.BlockSpec(memory_space=pltpu.VMEM)
ANY = pl.BlockSpec(memory_space=pl.ANY)


def shape(*dims, dtype=F32):
    return jax.ShapeDtypeStruct(dims, dtype)


def call(kernel, flops, out_shape, in_specs, out_specs, scratch):
    return pl.pallas_call(
        kernel,
        out_shape=out_shape,
        in_specs=in_specs,
        out_specs=out_specs,
        scratch_shapes=scratch,
        compiler_params=pltpu.CompilerParams(vmem_limit_bytes=24 * 1024 * 1024),
        cost_estimate=pl.CostEstimate(flops=flops, bytes_accessed=1, transcendentals=0),
    )


def body(left_blocks, left_rows, left_cols, left_counts, right_blocks, right_cols):
    left = left_blocks[0, 0]
    right = jnp.swapaxes(right_blocks[0, 0], 0, 1)
    kcols = jnp.swapaxes(right_cols[:, 0], 1, 2)
    l2, l1 = from_behind(left, "col", -2), from_behind(left, "col", -1)
    r2 = from_behind(right, "row", -2)
    sums = shape(QUADS, RB * 24, 128)
    dense_left = shape(2 * ROWS, DEPTH, dtype=BF16)
    dense_right = shape(DEPTH, WIDE, dtype=BF16)
    w_scratch = pltpu.VMEM((552, 128), F32)
    a0, b0, r0, spread_t, pick, mask, spread = call(
        first_kernel, 1,
        (
            dense_left, dense_right, shape(NB, 128, dtype=BF16), shape(AT[-1], 256, dtype=BF16),
            shape(3, 4 * RB, SA, dtype=BF16), shape(3, SA, 256, dtype=BF16), shape(3, 4, KB * BPK, KB * CB, dtype=BF16),
        ),
        [ANY] * 6, (VMEM,) * 7,
        [
            pltpu.SMEM(left_counts.shape, jnp.int32),
            pltpu.VMEM(left_rows.shape, jnp.int32),
            pltpu.VMEM(left_cols.shape, jnp.int32),
            pltpu.VMEM(kcols.shape, jnp.int32),
            pltpu.VMEM((SA, NB), BF16),
            w_scratch,
            pltpu.SemaphoreType.DMA((6,)),
        ],
    )(*(pltpu.with_memory_space_constraint(x, pltpu.HBM) for x in (left_counts, left_rows, left_cols, kcols, left, right)))
    relay = call(relay_kernel, 10**10, shape(NB, 128, dtype=BF16), [VMEM] * 2 + [ANY], VMEM, [])(r0, r2, a0)
    r1 = lax.ppermute(relay, "row", [(i, i ^ 1) for i in range(lax.axis_size("row"))])
    b2, before = call(
        far_right_kernel, 10**10, (dense_right, sums), [VMEM] * 4 + [ANY], (VMEM,) * 2, [w_scratch],
    )(r2, spread, a0, b0, relay)
    out = call(
        last_kernel, 10**10, shape(NB, 1, RB * CB), [VMEM] * 9, ANY,
        [
            pltpu.VMEM(dense_left.shape, BF16),
            pltpu.VMEM(dense_left.shape, BF16),
            pltpu.VMEM(dense_right.shape, BF16),
            w_scratch,
            pltpu.VMEM(sums.shape, F32),
            pltpu.VMEM((3, QUADS, 4, 4, 8, 128), F32),
            pltpu.VMEM((2120, 128), F32),
            pltpu.SemaphoreType.DMA((3,)),
        ],
    )(l2, l1, r1, spread_t, pick, mask, spread, b2, before)
    return jnp.transpose(out[None], (0, 2, 3, 1))


def solution(mesh):
    in_specs = (
        P("row", "col", None, None),
        P("row", None, None),
        P("row", None, None),
        P("row", None),
        P("row", "col", None, None),
        P(None, "col", None, None),
    )
    out_specs = P("row", "col", None, None)
    return jax.shard_map(body, mesh=mesh, in_specs=in_specs, out_specs=out_specs, check_vma=False)
```

time: 17.4 us -> 15.4 us (0.89)
  Pallas kernels: 9.36 us -> 7.07 us
  waiting for transfers between devices: 0.01 us -> 0.22 us
    pallas_call x5 -> x4, Pallas kernels: 9.36 us -> 7.07 us  [the longest x1 3.72 us: body(): call(last_kernel, 10 ** 10, shape(NB, 1, RB * CB), [VMEM] * 9, ANY, [pltp...]
    ppermute x0 -> x1, waiting for transfers between devices: none -> 0.22 us  [body(): lax.ppermute(relay, 'row', [(i, i ^ 1) for i in range(lax.axis_size('row'...]
    ppermute x4 -> x3, starting transfers between devices: 7.83 us -> 7.83 us  [from_behind(): lax.ppermute(value, axis, [(i, (i + by) % devices) for i in range(devices)])]
  transfers between devices with their start and end apart: 4 -> 4, of which waited for: 0 -> 1; matrix products, arithmetic and copies ran while one was open for 0% -> 0% of each run, Pallas kernels for 35% -> 22%
where the time goes in v4:
time: 15.4 us; the launch traced here: 15.3 us
  starting transfers between devices  7.9 us (51%)
  Pallas kernels  7.07 us (46%)
  waiting for transfers between devices  0.22 us (1%)
    ppermute x3, starting transfers between devices, from_behind(): lax.ppermute(value, axis, [(i, (i + by) % devices) for i in range(devices)])  7.83 us
    pallas_call x1, Pallas kernels, body(): call(last_kernel, 10 ** 10, shape(NB, 1, RB * CB), [VMEM] * 9, ANY, [pltp...  3.72 us
    pallas_call x1, Pallas kernels, body(): call(first_kernel, 1, (dense_left, dense_right, shape(NB, 128, dtype=BF16...  2.22 us
    pallas_call x1, Pallas kernels, body(): call(far_right_kernel, 10 ** 10, (dense_right, sums), [VMEM] * 4 + [ANY],...  1.1 us
  transfers between devices with their start and end apart: 4, of which 1 were waited for; matrix products, arithmetic and copies ran while one was open for 0% of the time, Pallas kernels for 22%

profile of v4, /device:TPU:0, one launch (start us, length us, event | category | flops | bytes accessed | tf_op | source)
XLA Modules:
  0.0 15.3 jit_solution(9370047694582535014)
XLA Ops:
  0.0 3.9 %collective-permute-start.2 = (bf16[529,128]{1,0:T(8,128)(2,1)}, bf16[529,128]{1,0:T(8,128)(2,1)S(1)}, u32[]{:S(2)}, u32[]{:S(2)}) collective-permute-start(bf16[529,128]{1,0:T(8,128)(2,1)} %bitcast.10), channel_id=1, source_target_pairs={{0,24},{4,28},{8,0},{12,4},{16,8},{20,12},{24,16},{28,20},{1,25},{... | collective-permute-start | bytes 406280 | tf_op jit(solution)/shard_map/ppermute | solution.py:30
  3.9 2.6 %collective-permute-start = (bf16[64,529]{1,0:T(8,128)(2,1)}, bf16[64,529]{1,0:T(8,128)(2,1)S(1)}, u32[]{:S(2)}, u32[]{:S(2)}) collective-permute-start(bf16[64,529]{1,0:T(8,128)(2,1)} %bitcast.12), channel_id=1, source_target_pairs={{0,2},{1,3},{2,0},{3,1},{4,6},{5,7},{6,4},{7,5},{8,10},{9,11},{10,... | collective-permute-start | bytes 203144 | tf_op jit(solution)/shard_map/ppermute | solution.py:30
  6.5 1.3 %collective-permute-start.1 = (bf16[64,529]{1,0:T(8,128)(2,1)}, bf16[64,529]{1,0:T(8,128)(2,1)S(1)}, u32[]{:S(2)}, u32[]{:S(2)}) collective-permute-start(bf16[64,529]{1,0:T(8,128)(2,1)} %bitcast.13), channel_id=1, source_target_pairs={{0,3},{1,0},{2,1},{3,2},{4,7},{5,4},{6,5},{7,6},{8,11},{9,8},{10,9... | collective-permute-start | bytes 203144 | tf_op jit(solution)/shard_map/ppermute | solution.py:30
  7.8 2.2 %shard_map.64 = (bf16[736,512]{1,0:T(8,128)(2,1)S(1)}, bf16[512,768]{1,0:T(8,128)(2,1)S(1)}, bf16[529,128]{1,0:T(8,128)(2,1)S(1)}, bf16[1937,256]{1,0:T(8,128)(2...) custom-call(s32[1,4]{1,0:T(1,128)} %counts_hbm.1, ...), custom_call_target="tpu_custom_call" | custom-call | flops 1 | bytes 1 | tf_op jit(solution)/shard_map/pallas_call | solution.py:247
  10.1 0.0 collective-permute-done.2.r2.r
  10.1 0.1 collective-permute-start.3
  10.2 1.1 %shard_map.66 = (bf16[512,768]{1,0:T(8,128)(2,1)S(1)}, f32[6,384,128]{2,1,0:T(8,128)S(1)}) custom-call(bf16[529,128]{1,0:T(8,128)(2,1)S(1)} %collective-permute-done.2.r2.r, bf16[3,4,128,512]{3,2,1,0:T(8,128)(2,1)S(1)} %get-tuple-element.19.spread_ref, bf16[736,512]{1,0:T(8,128)(2,1)S(1)} %get-tuple-element.15._.a0, ...), custom_call_target="tpu_custom_call" | custom-call | flops 10000000000 | bytes 1 | tf_op jit(solution)/shard_map/pallas_call | solution.py:266
  11.3 0.0 collective-permute-done.l2
  11.3 0.0 collective-permute-done.1.l1
  11.3 0.2 %collective-permute-done.3.r1 = bf16[529,128]{1,0:T(8,128)(2,1)S(1)} collective-permute-done((bf16[529,128]{1,0:T(8,128)(2,1)S(1)}, bf16[529,128]{1,0:T(8,128)(2,1)S(1)}, u32[]{:S(2)}, u32[]{:S(2)}) %collective-permute-start.3) | collective-permute-done | bytes 135456 | tf_op jit(solution)/shard_map/ppermute | solution.py:265
  11.5 3.7 %shard_map.67 = f32[529,1,512]{2,1,0:T(1,128)} custom-call(bf16[64,529]{1,0:T(8,128)(2,1)S(1)} %collective-permute-done.l2, bf16[64,529]{1,0:T(8,128)(2,1)S(1)} %collective-permute-done.1.l1, bf16[529,128]{1,0:T(8,128)(2,1)S(1)} %collective-permute-done.3.r1, bf16[1937,256]{1,0:T(8,128)(2,1)S(1)} %get-tuple-element.16.t_ref, ...), custom_call_target="tpu_custom_call" | custom-call | flops 10000000000 | bytes 1 | tf_op jit(solution)/shard_map/pallas_call | solution.py:269
  (1 shorter events, 0.0 us)
Async XLA Ops:
  0.0 10.1 %collective-permute-start.2 = (bf16[529,128]{1,0:T(8,128)(2,1)}, bf16[529,128]{1,0:T(8,128)(2,1)S(1)}, u32[]{:S(2)}, u32[]{:S(2)}) collective-permute-start(bf16[529,128]{1,0:T(8,128)(2,1)} %bitcast.10), channel_id=1, source_target_pairs={{0,24},{4,28},{8,0},{12,4},{16,8},{20,12},{24,16},{28,20},{1,25},{... | collective-permute-start | bytes 406280 | tf_op jit(solution)/shard_map/ppermute | solution.py:30
  3.9 7.4 %collective-permute-start = (bf16[64,529]{1,0:T(8,128)(2,1)}, bf16[64,529]{1,0:T(8,128)(2,1)S(1)}, u32[]{:S(2)}, u32[]{:S(2)}) collective-permute-start(bf16[64,529]{1,0:T(8,128)(2,1)} %bitcast.12), channel_id=1, source_target_pairs={{0,2},{1,3},{2,0},{3,1},{4,6},{5,7},{6,4},{7,5},{8,10},{9,11},{10,... | collective-permute-start | bytes 203144 | tf_op jit(solution)/shard_map/ppermute | solution.py:30
  6.5 4.8 %collective-permute-start.1 = (bf16[64,529]{1,0:T(8,128)(2,1)}, bf16[64,529]{1,0:T(8,128)(2,1)S(1)}, u32[]{:S(2)}, u32[]{:S(2)}) collective-permute-start(bf16[64,529]{1,0:T(8,128)(2,1)} %bitcast.13), channel_id=1, source_target_pairs={{0,3},{1,0},{2,1},{3,2},{4,7},{5,4},{6,5},{7,6},{8,11},{9,8},{10,9... | collective-permute-start | bytes 203144 | tf_op jit(solution)/shard_map/ppermute | solution.py:30
  10.1 1.4 %collective-permute-start.3 = (bf16[529,128]{1,0:T(8,128)(2,1)S(1)}, bf16[529,128]{1,0:T(8,128)(2,1)S(1)}, u32[]{:S(2)}, u32[]{:S(2)}) collective-permute-start(bf16[529,128]{1,0:T(8,128)(2,1)S(1)} %shard_map.65._), channel_id=1, source_target_pairs={{0,4},{4,0},{8,12},{12,8},{16,20},{20,16},{24,28},{28,24},{1,5},{5... | collective-permute-start | bytes 406280 | tf_op jit(solution)/shard_map/ppermute | solution.py:265

commit v5 on v4

--- a/solution.py
+++ b/solution.py
@@ -94,7 +94,7 @@
                 for g in range(KB // 4):
                     rows, lanes = slice(g * RB, (g + 1) * RB), slice(h * 128, (h + 1) * 128)
                     a_ref[i * RB : (i + 1) * RB, g * 128 : (g + 1) * 128] = hi[rows, lanes]
-                    a_ref[(BS + i) * RB : (BS + i + 1) * RB, g * 128 : (g + 1) * 128] = lo[rows, lanes]
+                    a_ref[i * RB : (i + 1) * RB, DEPTH + g * 128 : DEPTH + (g + 1) * 128] = lo[rows, lanes]
 
 
 def right_panel(r_ref, spread_ref, w_ref, b_ref):
@@ -122,8 +122,12 @@
 
 
 def product(panels, u):
-    both = sum(jnp.dot(a[...], b[:, 256 * u : 256 * (u + 1)], preferred_element_type=F32) for a, b in panels)
-    return both[:ROWS] + both[ROWS:]
+    total = None
+    for a, b in panels:
+        for part in range(2):
+            one = jnp.dot(a[:, part * DEPTH : (part + 1) * DEPTH], b[:, 256 * u : 256 * (u + 1)], preferred_element_type=F32)
+            total = one if total is None else total + one
+    return total
 
 
 def put_rows(p_ref, add_ref, total, u):
@@ -241,7 +245,7 @@
     l2, l1 = from_behind(left, "col", -2), from_behind(left, "col", -1)
     r2 = from_behind(right, "row", -2)
     sums = shape(QUADS, RB * 24, 128)
-    dense_left = shape(2 * ROWS, DEPTH, dtype=BF16)
+    dense_left = shape(ROWS, 2 * DEPTH, dtype=BF16)
     dense_right = shape(DEPTH, WIDE, dtype=BF16)
     w_scratch = pltpu.VMEM((552, 128), F32)
     a0, b0, r0, spread_t, pick, mask, spread = call(

time: 15.4 us -> 15.3 us (level)
  transfers between devices with their start and end apart: 4 -> 4, of which waited for: 1 -> 1; matrix products, arithmetic and copies ran while one was open for 0% -> 0% of each run, Pallas kernels for 22% -> 23%
where the time goes in v5:
time: 15.3 us; the launch traced here: 15.1 us
  starting transfers between devices  7.9 us (52%)
  Pallas kernels  7 us (46%)
  waiting for transfers between devices  0.17 us (1%)
    ppermute x3, starting transfers between devices, from_behind(): lax.ppermute(value, axis, [(i, (i + by) % devices) for i in range(devices)])  7.83 us
    pallas_call x1, Pallas kernels, body(): call(last_kernel, 10 ** 10, shape(NB, 1, RB * CB), [VMEM] * 9, ANY, [pltp...  3.59 us
    pallas_call x1, Pallas kernels, body(): call(first_kernel, 1, (dense_left, dense_right, shape(NB, 128, dtype=BF16...  2.22 us
    pallas_call x1, Pallas kernels, body(): call(far_right_kernel, 10 ** 10, (dense_right, sums), [VMEM] * 4 + [ANY],...  1.15 us
  transfers between devices with their start and end apart: 4, of which 1 were waited for; matrix products, arithmetic and copies ran while one was open for 0% of the time, Pallas kernels for 23%

profile of v5, /device:TPU:0, one launch (start us, length us, event | category | flops | bytes accessed | tf_op | source)
XLA Modules:
  0.0 15.1 jit_solution(4293675903752825479)
XLA Ops:
  0.0 3.9 %collective-permute-start.2 = (bf16[529,128]{1,0:T(8,128)(2,1)}, bf16[529,128]{1,0:T(8,128)(2,1)S(1)}, u32[]{:S(2)}, u32[]{:S(2)}) collective-permute-start(bf16[529,128]{1,0:T(8,128)(2,1)} %bitcast.10), channel_id=1, source_target_pairs={{0,24},{4,28},{8,0},{12,4},{16,8},{20,12},{24,16},{28,20},{1,25},{... | collective-permute-start | bytes 406280 | tf_op jit(solution)/shard_map/ppermute | solution.py:30
  3.9 2.6 %collective-permute-start = (bf16[64,529]{1,0:T(8,128)(2,1)}, bf16[64,529]{1,0:T(8,128)(2,1)S(1)}, u32[]{:S(2)}, u32[]{:S(2)}) collective-permute-start(bf16[64,529]{1,0:T(8,128)(2,1)} %bitcast.12), channel_id=1, source_target_pairs={{0,2},{1,3},{2,0},{3,1},{4,6},{5,7},{6,4},{7,5},{8,10},{9,11},{10,... | collective-permute-start | bytes 203144 | tf_op jit(solution)/shard_map/ppermute | solution.py:30
  6.5 1.3 %collective-permute-start.1 = (bf16[64,529]{1,0:T(8,128)(2,1)}, bf16[64,529]{1,0:T(8,128)(2,1)S(1)}, u32[]{:S(2)}, u32[]{:S(2)}) collective-permute-start(bf16[64,529]{1,0:T(8,128)(2,1)} %bitcast.13), channel_id=1, source_target_pairs={{0,3},{1,0},{2,1},{3,2},{4,7},{5,4},{6,5},{7,6},{8,11},{9,8},{10,9... | collective-permute-start | bytes 203144 | tf_op jit(solution)/shard_map/ppermute | solution.py:30
  7.8 2.2 %shard_map.64 = (bf16[368,1024]{1,0:T(8,128)(2,1)S(1)}, bf16[512,768]{1,0:T(8,128)(2,1)S(1)}, bf16[529,128]{1,0:T(8,128)(2,1)S(1)}, bf16[1937,256]{1,0:T(8,128)(...) custom-call(s32[1,4]{1,0:T(1,128)} %counts_hbm.1, ...), custom_call_target="tpu_custom_call" | custom-call | flops 1 | bytes 1 | tf_op jit(solution)/shard_map/pallas_call | solution.py:251
  10.1 0.0 collective-permute-done.2.r2.r
  10.1 0.1 collective-permute-start.3
  10.2 1.1 %shard_map.66 = (bf16[512,768]{1,0:T(8,128)(2,1)S(1)}, f32[6,384,128]{2,1,0:T(8,128)S(1)}) custom-call(bf16[529,128]{1,0:T(8,128)(2,1)S(1)} %collective-permute-done.2.r2.r, bf16[3,4,128,512]{3,2,1,0:T(8,128)(2,1)S(1)} %get-tuple-element.19.spread_ref, bf16[368,1024]{1,0:T(8,128)(2,1)S(1)} %get-tuple-element.15._.a0, ...), custom_call_target="tpu_custom_call" | custom-call | flops 10000000000 | bytes 1 | tf_op jit(solution)/shard_map/pallas_call | solution.py:270
  11.3 0.0 collective-permute-done.l2
  11.4 0.0 collective-permute-done.1.l1
  11.4 0.2 %collective-permute-done.3.r1 = bf16[529,128]{1,0:T(8,128)(2,1)S(1)} collective-permute-done((bf16[529,128]{1,0:T(8,128)(2,1)S(1)}, bf16[529,128]{1,0:T(8,128)(2,1)S(1)}, u32[]{:S(2)}, u32[]{:S(2)}) %collective-permute-start.3) | collective-permute-done | bytes 135456 | tf_op jit(solution)/shard_map/ppermute | solution.py:269
  11.5 3.6 %shard_map.67 = f32[529,1,512]{2,1,0:T(1,128)} custom-call(bf16[64,529]{1,0:T(8,128)(2,1)S(1)} %collective-permute-done.l2, bf16[64,529]{1,0:T(8,128)(2,1)S(1)} %collective-permute-done.1.l1, bf16[529,128]{1,0:T(8,128)(2,1)S(1)} %collective-permute-done.3.r1, bf16[1937,256]{1,0:T(8,128)(2,1)S(1)} %get-tuple-element.16.t_ref, ...), custom_call_target="tpu_custom_call" | custom-call | flops 10000000000 | bytes 1 | tf_op jit(solution)/shard_map/pallas_call | solution.py:273
  (1 shorter events, 0.0 us)
Async XLA Ops:
  0.0 10.1 %collective-permute-start.2 = (bf16[529,128]{1,0:T(8,128)(2,1)}, bf16[529,128]{1,0:T(8,128)(2,1)S(1)}, u32[]{:S(2)}, u32[]{:S(2)}) collective-permute-start(bf16[529,128]{1,0:T(8,128)(2,1)} %bitcast.10), channel_id=1, source_target_pairs={{0,24},{4,28},{8,0},{12,4},{16,8},{20,12},{24,16},{28,20},{1,25},{... | collective-permute-start | bytes 406280 | tf_op jit(solution)/shard_map/ppermute | solution.py:30
  3.9 7.5 %collective-permute-start = (bf16[64,529]{1,0:T(8,128)(2,1)}, bf16[64,529]{1,0:T(8,128)(2,1)S(1)}, u32[]{:S(2)}, u32[]{:S(2)}) collective-permute-start(bf16[64,529]{1,0:T(8,128)(2,1)} %bitcast.12), channel_id=1, source_target_pairs={{0,2},{1,3},{2,0},{3,1},{4,6},{5,7},{6,4},{7,5},{8,10},{9,11},{10,... | collective-permute-start | bytes 203144 | tf_op jit(solution)/shard_map/ppermute | solution.py:30
  6.5 4.9 %collective-permute-start.1 = (bf16[64,529]{1,0:T(8,128)(2,1)}, bf16[64,529]{1,0:T(8,128)(2,1)S(1)}, u32[]{:S(2)}, u32[]{:S(2)}) collective-permute-start(bf16[64,529]{1,0:T(8,128)(2,1)} %bitcast.13), channel_id=1, source_target_pairs={{0,3},{1,0},{2,1},{3,2},{4,7},{5,4},{6,5},{7,6},{8,11},{9,8},{10,9... | collective-permute-start | bytes 203144 | tf_op jit(solution)/shard_map/ppermute | solution.py:30
  10.1 1.4 %collective-permute-start.3 = (bf16[529,128]{1,0:T(8,128)(2,1)S(1)}, bf16[529,128]{1,0:T(8,128)(2,1)S(1)}, u32[]{:S(2)}, u32[]{:S(2)}) collective-permute-start(bf16[529,128]{1,0:T(8,128)(2,1)S(1)} %shard_map.65._), channel_id=1, source_target_pairs={{0,4},{4,0},{8,12},{12,8},{16,20},{20,16},{24,28},{28,24},{1,5},{5... | collective-permute-start | bytes 406280 | tf_op jit(solution)/shard_map/ppermute | solution.py:269

commit v6 on v5

--- a/solution.py
+++ b/solution.py
@@ -51,9 +51,12 @@
         t_ref[AT[u] : AT[u + 1], :] = jnp.where(entry == source, 1.0, 0.0).astype(BF16)
 
 
-def slot_pick(rows, cols, count):
+def slot_code(rows, cols, count):
     slot = lax.broadcasted_iota(jnp.int32, (1, SA), 1)
-    code = jnp.where(slot < count, (cols >> 2) * RB + rows, -1)
+    return jnp.where(slot < count, (cols >> 2) * RB + rows, -1)
+
+
+def slot_pick(code):
     place = lax.broadcasted_iota(jnp.int32, (4 * RB, SA), 0)
     return jnp.where(place == code, 1.0, 0.0).astype(BF16)
 
@@ -79,7 +82,9 @@
         spread_ref[turn] = jnp.concatenate(spread, axis=0).astype(BF16)
 
 
-def left_panel(l_ref, pick, mask, t_ref, a_ref):
+def left_panel(l_ref, slots_ref, s, t_ref, a_ref):
+    pick = slot_pick(slots_ref[s : s + 1])
+    mask = slot_mask(slots_ref[s + 3 : s + 4])
     wide = []
     for u, (start, stop) in enumerate(SPANS):
         copies = jnp.dot(l_ref[:, start:stop], t_ref[AT[u] : AT[u + 1], :], preferred_element_type=F32)
@@ -139,8 +144,8 @@
 
 
 def first_kernel(counts_hbm, rows_hbm, cols_hbm, kcols_hbm, l_hbm, r_hbm,
-                 a_ref, b_ref, r_ref, t_ref, pick_ref, mask_ref, spread_ref,
-                 counts, rows, cols, kcols, l_ref, w_ref, sems):
+                 a_ref, b_ref, r_ref, t_ref, slots_ref, near_ref,
+                 counts, rows, cols, kcols, l_ref, w_ref, spread_ref, sems):
     moves = [
         pltpu.make_async_copy(s, d, sems.at[n])
         for n, (s, d) in enumerate((
@@ -158,11 +163,12 @@
         panel = lax.rem(lax.axis_index("col") + s, ncol)
         source = lax.rem(lax.axis_index("row") + s, nrow)
         panel_cols = cols[0, pl.ds(panel, 1), :]
-        pick_ref[s] = slot_pick(rows[0, pl.ds(panel, 1), :], panel_cols, counts[0, panel])
-        mask_ref[s] = slot_mask(panel_cols)
-        column_spread(kcols[source], spread_ref.at[s])
-    right_panel(r_ref, spread_ref.at[0], w_ref, b_ref)
-    left_panel(l_ref, pick_ref[0], mask_ref[0], t_ref, a_ref)
+        slots_ref[s : s + 1] = slot_code(rows[0, pl.ds(panel, 1), :], panel_cols, counts[0, panel])
+        slots_ref[s + 3 : s + 4] = panel_cols
+        near_ref[s] = kcols[source]
+    column_spread(near_ref[0], spread_ref)
+    right_panel(r_ref, spread_ref, w_ref, b_ref)
+    left_panel(l_ref, slots_ref, 0, t_ref, a_ref)
 
 
 def relay_kernel(r0, r2, _, x_ref):
@@ -177,16 +183,18 @@
         x_ref[...] = r2[...]
 
 
-def far_right_kernel(r, spread_ref, a0, b0, _, b_ref, p_ref, w_ref):
-    right_panel(r, spread_ref.at[2], w_ref, b_ref)
+def far_right_kernel(r, near_ref, a0, b0, _, b_ref, p_ref, w_ref, spread_ref):
+    column_spread(near_ref[2], spread_ref)
+    right_panel(r, spread_ref, w_ref, b_ref)
     for u in range(3):
         put_rows(p_ref, None, product(((a0, b0),), u), u)
 
 
-def last_kernel(l2, l1, r1, t_ref, pick_ref, mask_ref, spread_ref, b2, before_ref, out_hbm, a2, a1, b1, w_ref, p_ref, h_ref, o_ref, sems):
-    left_panel(l2, pick_ref[2], mask_ref[2], t_ref, a2)
-    left_panel(l1, pick_ref[1], mask_ref[1], t_ref, a1)
-    right_panel(r1, spread_ref.at[1], w_ref, b1)
+def last_kernel(l2, l1, r1, t_ref, slots_ref, near_ref, b2, before_ref, out_hbm, a2, a1, b1, w_ref, spread_ref, p_ref, h_ref, o_ref, sems):
+    left_panel(l2, slots_ref, 2, t_ref, a2)
+    left_panel(l1, slots_ref, 1, t_ref, a1)
+    column_spread(near_ref[1], spread_ref)
+    right_panel(r1, spread_ref, w_ref, b1)
     out = out_hbm.reshape(NB * 4, 128)
     moves = []
     for u in range(3):
@@ -198,8 +206,9 @@
                 v = [p_ref[q, t : t + 8, :] for t in at]
                 half = lanes_like(v[0]) < 64
                 for a in (0, 1):
-                    h_ref[ib, q, rq, a] = jnp.where(half, v[a], pltpu.roll(v[a + 2], 64, 1))
-                    h_ref[ib, q, rq, a + 2] = jnp.where(half, pltpu.roll(v[a], 64, 1), v[a + 2])
+                    crossed = pltpu.roll(jnp.where(half, v[a + 2], v[a]), 64, 1)
+                    h_ref[ib, q, rq, a] = jnp.where(half, v[a], crossed)
+                    h_ref[ib, q, rq, a + 2] = jnp.where(half, crossed, v[a + 2])
             for q, rq, ib in places:
                 n = 8 if ib < 2 else 7
                 for a in (0, 2):
@@ -248,41 +257,42 @@
     dense_left = shape(ROWS, 2 * DEPTH, dtype=BF16)
     dense_right = shape(DEPTH, WIDE, dtype=BF16)
     w_scratch = pltpu.VMEM((552, 128), F32)
-    a0, b0, r0, spread_t, pick, mask, spread = call(
+    spread_scratch = pltpu.VMEM((4, KB * BPK, KB * CB), BF16)
+    a0, b0, r0, spread_t, slots, near = call(
         first_kernel, 1,
         (
             dense_left, dense_right, shape(NB, 128, dtype=BF16), shape(AT[-1], 256, dtype=BF16),
-            shape(3, 4 * RB, SA, dtype=BF16), shape(3, SA, 256, dtype=BF16), shape(3, 4, KB * BPK, KB * CB, dtype=BF16),
+            shape(8, SA, dtype=jnp.int32), shape(3, BPK, KB, dtype=jnp.int32),
         ),
-        [ANY] * 6, (VMEM,) * 7,
+        [ANY] * 6, (VMEM,) * 6,
         [
             pltpu.SMEM(left_counts.shape, jnp.int32),
             pltpu.VMEM(left_rows.shape, jnp.int32),
             pltpu.VMEM(left_cols.shape, jnp.int32),
             pltpu.VMEM(kcols.shape, jnp.int32),
             pltpu.VMEM((SA, NB), BF16),
-            w_scratch,
+            w_scratch, spread_scratch,
             pltpu.SemaphoreType.DMA((6,)),
         ],
     )(*(pltpu.with_memory_space_constraint(x, pltpu.HBM) for x in (left_counts, left_rows, left_cols, kcols, left, right)))
     relay = call(relay_kernel, 10**10, shape(NB, 128, dtype=BF16), [VMEM] * 2 + [ANY], VMEM, [])(r0, r2, a0)
     r1 = lax.ppermute(relay, "row", [(i, i ^ 1) for i in range(lax.axis_size("row"))])
     b2, before = call(
-        far_right_kernel, 10**10, (dense_right, sums), [VMEM] * 4 + [ANY], (VMEM,) * 2, [w_scratch],
-    )(r2, spread, a0, b0, relay)
+        far_right_kernel, 10**10, (dense_right, sums), [VMEM] * 4 + [ANY], (VMEM,) * 2, [w_scratch, spread_scratch],
+    )(r2, near, a0, b0, relay)
     out = call(
-        last_kernel, 10**10, shape(NB, 1, RB * CB), [VMEM] * 9, ANY,
+        last_kernel, 10**10, shape(NB, 1, RB * CB), [VMEM] * 8, ANY,
         [
             pltpu.VMEM(dense_left.shape, BF16),
             pltpu.VMEM(dense_left.shape, BF16),
             pltpu.VMEM(dense_right.shape, BF16),
-            w_scratch,
+            w_scratch, spread_scratch,
             pltpu.VMEM(sums.shape, F32),
             pltpu.VMEM((3, QUADS, 4, 4, 8, 128), F32),
             pltpu.VMEM((2120, 128), F32),
             pltpu.SemaphoreType.DMA((3,)),
         ],
-    )(l2, l1, r1, spread_t, pick, mask, spread, b2, before)
+    )(l2, l1, r1, spread_t, slots, near, b2, before)
     return jnp.transpose(out[None], (0, 2, 3, 1))
 
 

time: 15.3 us -> 15.2 us (level)
    pallas_call x1, Pallas kernels: 2.22 us -> 1.94 us  [body(): call(first_kernel, 1, (dense_left, dense_right, shape(NB, 128, dtype=BF16...]
    ppermute x1, waiting for transfers between devices: 0.17 us -> 0.01 us  [body(): lax.ppermute(relay, 'row', [(i, i ^ 1) for i in range(lax.axis_size('row'...]
    ppermute x3, waiting for transfers between devices: 0.01 us -> 0.16 us  [from_behind(): lax.ppermute(value, axis, [(i, (i + by) % devices) for i in range(devices)])]
  transfers between devices with their start and end apart: 4 -> 4, of which waited for: 1 -> 1; matrix products, arithmetic and copies ran while one was open for 0% -> 0% of each run, Pallas kernels for 23% -> 21%
where the time goes in v6:
time: 15.2 us; the launch traced here: 15 us
  starting transfers between devices  7.9 us (52%)
  Pallas kernels  6.92 us (46%)
  waiting for transfers between devices  0.17 us (1%)
    ppermute x3, starting transfers between devices, from_behind(): lax.ppermute(value, axis, [(i, (i + by) % devices) for i in range(devices)])  7.83 us
    pallas_call x1, Pallas kernels, body(): call(last_kernel, 10 ** 10, shape(NB, 1, RB * CB), [VMEM] * 8, ANY, [pltp...  3.74 us
    pallas_call x1, Pallas kernels, body(): call(first_kernel, 1, (dense_left, dense_right, shape(NB, 128, dtype=BF16...  1.94 us
    pallas_call x1, Pallas kernels, body(): call(far_right_kernel, 10 ** 10, (dense_right, sums), [VMEM] * 4 + [ANY],...  1.21 us
  transfers between devices with their start and end apart: 4, of which 1 were waited for; matrix products, arithmetic and copies ran while one was open for 0% of the time, Pallas kernels for 21%

profile of v6, /device:TPU:0, one launch (start us, length us, event | category | flops | bytes accessed | tf_op | source)
XLA Modules:
  0.0 15.0 jit_solution(16359950529140683245)
XLA Ops:
  0.0 3.9 %collective-permute-start.2 = (bf16[529,128]{1,0:T(8,128)(2,1)}, bf16[529,128]{1,0:T(8,128)(2,1)S(1)}, u32[]{:S(2)}, u32[]{:S(2)}) collective-permute-start(bf16[529,128]{1,0:T(8,128)(2,1)} %bitcast.10), channel_id=1, source_target_pairs={{0,24},{4,28},{8,0},{12,4},{16,8},{20,12},{24,16},{28,20},{1,25},{... | collective-permute-start | bytes 406280 | tf_op jit(solution)/shard_map/ppermute | solution.py:30
  3.9 2.6 %collective-permute-start = (bf16[64,529]{1,0:T(8,128)(2,1)}, bf16[64,529]{1,0:T(8,128)(2,1)S(1)}, u32[]{:S(2)}, u32[]{:S(2)}) collective-permute-start(bf16[64,529]{1,0:T(8,128)(2,1)} %bitcast.12), channel_id=1, source_target_pairs={{0,2},{1,3},{2,0},{3,1},{4,6},{5,7},{6,4},{7,5},{8,10},{9,11},{10,... | collective-permute-start | bytes 203144 | tf_op jit(solution)/shard_map/ppermute | solution.py:30
  6.5 1.3 %collective-permute-start.1 = (bf16[64,529]{1,0:T(8,128)(2,1)}, bf16[64,529]{1,0:T(8,128)(2,1)S(1)}, u32[]{:S(2)}, u32[]{:S(2)}) collective-permute-start(bf16[64,529]{1,0:T(8,128)(2,1)} %bitcast.13), channel_id=1, source_target_pairs={{0,3},{1,0},{2,1},{3,2},{4,7},{5,4},{6,5},{7,6},{8,11},{9,8},{10,9... | collective-permute-start | bytes 203144 | tf_op jit(solution)/shard_map/ppermute | solution.py:30
  7.8 1.9 %shard_map.64 = (bf16[368,1024]{1,0:T(8,128)(2,1)S(1)}, bf16[512,768]{1,0:T(8,128)(2,1)S(1)}, bf16[529,128]{1,0:T(8,128)(2,1)S(1)}, bf16[1937,256]{1,0:T(8,128)(...) custom-call(s32[1,4]{1,0:T(1,128)} %counts_hbm.1, s32[1,4,64]{2,1,0:T(4,128)} %rows_hbm.1, s32[1,4,64]{2,1,0:T(4,128)} %cols_hbm.1, ...), custom_call_target="tpu_custom_call" | custom-call | flops 1 | bytes 1 | tf_op jit(solution)/shard_map/pallas_call | solution.py:261
  9.8 0.0 collective-permute-done.2.r2.r
  9.8 0.1 collective-permute-start.3
  9.9 1.2 %shard_map.66 = (bf16[512,768]{1,0:T(8,128)(2,1)S(1)}, f32[6,384,128]{2,1,0:T(8,128)S(1)}) custom-call(bf16[529,128]{1,0:T(8,128)(2,1)S(1)} %collective-permute-done.2.r2.r, s32[3,8,16]{2,1,0:T(8,128)S(1)} %get-tuple-element.17.near_ref, bf16[368,1024]{1,0:T(8,128)(2,1)S(1)} %get-tuple-element.14._.a0, bf16[512,768]{1,0:T(8,128)(2,1)S(1)} %get-tuple-element.18.b0, ...), custom_call_target="tpu_custom_call" | custom-call | flops 10000000000 | bytes 1 | tf_op jit(solution)/shard_map/pallas_call | solution.py:280
  11.1 0.0 collective-permute-done.l2
  11.1 0.1 collective-permute-done.1.l1
  11.3 0.0 collective-permute-done.3.r1
  11.3 3.7 %shard_map.67 = f32[529,1,512]{2,1,0:T(1,128)} custom-call(bf16[64,529]{1,0:T(8,128)(2,1)S(1)} %collective-permute-done.l2, bf16[64,529]{1,0:T(8,128)(2,1)S(1)} %collective-permute-done.1.l1, bf16[529,128]{1,0:T(8,128)(2,1)S(1)} %collective-permute-done.3.r1, bf16[1937,256]{1,0:T(8,128)(2,1)S(1)} %get-tuple-element.15.t_ref, ...), custom_call_target="tpu_custom_call" | custom-call | flops 10000000000 | bytes 1 | tf_op jit(solution)/shard_map/pallas_call | solution.py:283
  (1 shorter events, 0.0 us)
Async XLA Ops:
  0.0 9.8 %collective-permute-start.2 = (bf16[529,128]{1,0:T(8,128)(2,1)}, bf16[529,128]{1,0:T(8,128)(2,1)S(1)}, u32[]{:S(2)}, u32[]{:S(2)}) collective-permute-start(bf16[529,128]{1,0:T(8,128)(2,1)} %bitcast.10), channel_id=1, source_target_pairs={{0,24},{4,28},{8,0},{12,4},{16,8},{20,12},{24,16},{28,20},{1,25},{... | collective-permute-start | bytes 406280 | tf_op jit(solution)/shard_map/ppermute | solution.py:30
  3.9 7.2 %collective-permute-start = (bf16[64,529]{1,0:T(8,128)(2,1)}, bf16[64,529]{1,0:T(8,128)(2,1)S(1)}, u32[]{:S(2)}, u32[]{:S(2)}) collective-permute-start(bf16[64,529]{1,0:T(8,128)(2,1)} %bitcast.12), channel_id=1, source_target_pairs={{0,2},{1,3},{2,0},{3,1},{4,6},{5,7},{6,4},{7,5},{8,10},{9,11},{10,... | collective-permute-start | bytes 203144 | tf_op jit(solution)/shard_map/ppermute | solution.py:30
  6.5 4.8 %collective-permute-start.1 = (bf16[64,529]{1,0:T(8,128)(2,1)}, bf16[64,529]{1,0:T(8,128)(2,1)S(1)}, u32[]{:S(2)}, u32[]{:S(2)}) collective-permute-start(bf16[64,529]{1,0:T(8,128)(2,1)} %bitcast.13), channel_id=1, source_target_pairs={{0,3},{1,0},{2,1},{3,2},{4,7},{5,4},{6,5},{7,6},{8,11},{9,8},{10,9... | collective-permute-start | bytes 203144 | tf_op jit(solution)/shard_map/ppermute | solution.py:30
  9.8 1.5 %collective-permute-start.3 = (bf16[529,128]{1,0:T(8,128)(2,1)S(1)}, bf16[529,128]{1,0:T(8,128)(2,1)S(1)}, u32[]{:S(2)}, u32[]{:S(2)}) collective-permute-start(bf16[529,128]{1,0:T(8,128)(2,1)S(1)} %shard_map.65._), channel_id=1, source_target_pairs={{0,4},{4,0},{8,12},{12,8},{16,20},{20,16},{24,28},{28,24},{1,5},{5... | collective-permute-start | bytes 406280 | tf_op jit(solution)/shard_map/ppermute | solution.py:279

commit v7 on v6

--- a/solution.py
+++ b/solution.py
@@ -82,9 +82,7 @@
         spread_ref[turn] = jnp.concatenate(spread, axis=0).astype(BF16)
 
 
-def left_panel(l_ref, slots_ref, s, t_ref, a_ref):
-    pick = slot_pick(slots_ref[s : s + 1])
-    mask = slot_mask(slots_ref[s + 3 : s + 4])
+def left_panel(l_ref, pick, mask, t_ref, a_ref):
     wide = []
     for u, (start, stop) in enumerate(SPANS):
         copies = jnp.dot(l_ref[:, start:stop], t_ref[AT[u] : AT[u + 1], :], preferred_element_type=F32)
@@ -168,7 +166,7 @@
         near_ref[s] = kcols[source]
     column_spread(near_ref[0], spread_ref)
     right_panel(r_ref, spread_ref, w_ref, b_ref)
-    left_panel(l_ref, slots_ref, 0, t_ref, a_ref)
+    left_panel(l_ref, slot_pick(slots_ref[0:1]), slot_mask(slots_ref[3:4]), t_ref, a_ref)
 
 
 def relay_kernel(r0, r2, _, x_ref):
@@ -183,17 +181,20 @@
         x_ref[...] = r2[...]
 
 
-def far_right_kernel(r, near_ref, a0, b0, _, b_ref, p_ref, w_ref, spread_ref):
+def far_right_kernel(r, slots_ref, near_ref, a0, b0, _, b_ref, p_ref, pick_ref, mask_ref, near_spread_ref, w_ref, spread_ref):
+    for s in (1, 2):
+        pick_ref[s - 1] = slot_pick(slots_ref[s : s + 1])
+        mask_ref[s - 1] = slot_mask(slots_ref[s + 3 : s + 4])
+    column_spread(near_ref[1], near_spread_ref)
     column_spread(near_ref[2], spread_ref)
     right_panel(r, spread_ref, w_ref, b_ref)
     for u in range(3):
         put_rows(p_ref, None, product(((a0, b0),), u), u)
 
 
-def last_kernel(l2, l1, r1, t_ref, slots_ref, near_ref, b2, before_ref, out_hbm, a2, a1, b1, w_ref, spread_ref, p_ref, h_ref, o_ref, sems):
-    left_panel(l2, slots_ref, 2, t_ref, a2)
-    left_panel(l1, slots_ref, 1, t_ref, a1)
-    column_spread(near_ref[1], spread_ref)
+def last_kernel(l2, l1, r1, t_ref, pick_ref, mask_ref, spread_ref, b2, before_ref, out_hbm, a2, a1, b1, w_ref, p_ref, h_ref, o_ref, sems):
+    left_panel(l2, pick_ref[1], mask_ref[1], t_ref, a2)
+    left_panel(l1, pick_ref[0], mask_ref[0], t_ref, a1)
     right_panel(r1, spread_ref, w_ref, b1)
     out = out_hbm.reshape(NB * 4, 128)
     moves = []
@@ -277,22 +278,27 @@
     )(*(pltpu.with_memory_space_constraint(x, pltpu.HBM) for x in (left_counts, left_rows, left_cols, kcols, left, right)))
     relay = call(relay_kernel, 10**10, shape(NB, 128, dtype=BF16), [VMEM] * 2 + [ANY], VMEM, [])(r0, r2, a0)
     r1 = lax.ppermute(relay, "row", [(i, i ^ 1) for i in range(lax.axis_size("row"))])
-    b2, before = call(
-        far_right_kernel, 10**10, (dense_right, sums), [VMEM] * 4 + [ANY], (VMEM,) * 2, [w_scratch, spread_scratch],
-    )(r2, near, a0, b0, relay)
+    b2, before, pick, mask, near_spread = call(
+        far_right_kernel, 10**10,
+        (
+            dense_right, sums, shape(2, 4 * RB, SA, dtype=BF16), shape(2, SA, 256, dtype=BF16),
+            shape(*spread_scratch.shape, dtype=BF16),
+        ),
+        [VMEM] * 5 + [ANY], (VMEM,) * 5, [w_scratch, spread_scratch],
+    )(r2, slots, near, a0, b0, relay)
     out = call(
-        last_kernel, 10**10, shape(NB, 1, RB * CB), [VMEM] * 8, ANY,
+        last_kernel, 10**10, shape(NB, 1, RB * CB), [VMEM] * 9, ANY,
         [
             pltpu.VMEM(dense_left.shape, BF16),
             pltpu.VMEM(dense_left.shape, BF16),
             pltpu.VMEM(dense_right.shape, BF16),
-            w_scratch, spread_scratch,
+            w_scratch,
             pltpu.VMEM(sums.shape, F32),
             pltpu.VMEM((3, QUADS, 4, 4, 8, 128), F32),
             pltpu.VMEM((2120, 128), F32),
             pltpu.SemaphoreType.DMA((3,)),
         ],
-    )(l2, l1, r1, spread_t, slots, near, b2, before)
+    )(l2, l1, r1, spread_t, pick, mask, near_spread, b2, before)
     return jnp.transpose(out[None], (0, 2, 3, 1))
 
 

time: 15.2 us -> 15.1 us (level)
  transfers between devices with their start and end apart: 4 -> 4, of which waited for: 1 -> 0; matrix products, arithmetic and copies ran while one was open for 0% -> 0% of each run, Pallas kernels for 21% -> 22%
where the time goes in v7:
time: 15.1 us; the launch traced here: 14.9 us
  starting transfers between devices  7.9 us (52%)
  Pallas kernels  6.91 us (46%)
    ppermute x3, starting transfers between devices, from_behind(): lax.ppermute(value, axis, [(i, (i + by) % devices) for i in range(devices)])  7.83 us
    pallas_call x1, Pallas kernels, body(): call(last_kernel, 10 ** 10, shape(NB, 1, RB * CB), [VMEM] * 9, ANY, [pltp...  3.61 us
    pallas_call x1, Pallas kernels, body(): call(first_kernel, 1, (dense_left, dense_right, shape(NB, 128, dtype=BF16...  1.89 us
    pallas_call x1, Pallas kernels, body(): call(far_right_kernel, 10 ** 10, (dense_right, sums, shape(2, 4 * RB, SA,...  1.37 us
  transfers between devices with their start and end apart: 4, of which 0 were waited for; matrix products, arithmetic and copies ran while one was open for 0% of the time, Pallas kernels for 22%

profile of v7, /device:TPU:0, one launch (start us, length us, event | category | flops | bytes accessed | tf_op | source)
XLA Modules:
  0.0 14.9 jit_solution(12219780368548402729)
XLA Ops:
  0.0 3.9 %collective-permute-start.2 = (bf16[529,128]{1,0:T(8,128)(2,1)}, bf16[529,128]{1,0:T(8,128)(2,1)S(1)}, u32[]{:S(2)}, u32[]{:S(2)}) collective-permute-start(bf16[529,128]{1,0:T(8,128)(2,1)} %bitcast.10), channel_id=1, source_target_pairs={{0,24},{4,28},{8,0},{12,4},{16,8},{20,12},{24,16},{28,20},{1,25},{... | collective-permute-start | bytes 406280 | tf_op jit(solution)/shard_map/ppermute | solution.py:30
  3.9 2.6 %collective-permute-start = (bf16[64,529]{1,0:T(8,128)(2,1)}, bf16[64,529]{1,0:T(8,128)(2,1)S(1)}, u32[]{:S(2)}, u32[]{:S(2)}) collective-permute-start(bf16[64,529]{1,0:T(8,128)(2,1)} %bitcast.12), channel_id=1, source_target_pairs={{0,2},{1,3},{2,0},{3,1},{4,6},{5,7},{6,4},{7,5},{8,10},{9,11},{10,... | collective-permute-start | bytes 203144 | tf_op jit(solution)/shard_map/ppermute | solution.py:30
  6.5 1.3 %collective-permute-start.1 = (bf16[64,529]{1,0:T(8,128)(2,1)}, bf16[64,529]{1,0:T(8,128)(2,1)S(1)}, u32[]{:S(2)}, u32[]{:S(2)}) collective-permute-start(bf16[64,529]{1,0:T(8,128)(2,1)} %bitcast.13), channel_id=1, source_target_pairs={{0,3},{1,0},{2,1},{3,2},{4,7},{5,4},{6,5},{7,6},{8,11},{9,8},{10,9... | collective-permute-start | bytes 203144 | tf_op jit(solution)/shard_map/ppermute | solution.py:30
  7.8 1.9 %shard_map.64 = (bf16[368,1024]{1,0:T(8,128)(2,1)S(1)}, bf16[512,768]{1,0:T(8,128)(2,1)S(1)}, bf16[529,128]{1,0:T(8,128)(2,1)S(1)}, bf16[1937,256]{1,0:T(8,128)(...) custom-call(s32[1,4]{1,0:T(1,128)} %counts_hbm.1, s32[1,4,64]{2,1,0:T(4,128)} %rows_hbm.1, s32[1,4,64]{2,1,0:T(4,128)} %cols_hbm.1, ...), custom_call_target="tpu_custom_call" | custom-call | flops 1 | bytes 1 | tf_op jit(solution)/shard_map/pallas_call | solution.py:262
  9.7 0.0 collective-permute-done.2.r2.r
  9.8 0.1 collective-permute-start.3
  9.9 1.4 %shard_map.66 = (bf16[512,768]{1,0:T(8,128)(2,1)S(1)}, f32[6,384,128]{2,1,0:T(8,128)S(1)}, bf16[2,64,64]{2,1,0:T(8,128)(2,1)S(1)}, bf16[2,64,256]{2,1,0:T(8,128)(2,1)S(1)}, bf16[4,128,512]{2,1,0:T(8,128)(2,1)S(1)}) custom-call(bf16[529,128]{1,0:T(8,128)(2,1)S(1)} %collective-permute-done.2.r2.r, s32[8,64]{1,0:T(8,128)S(1)} %get-tuple-element.19.slots_ref, ...), custom_call_target="tpu_custom_call" | custom-call | flops 10000000000 | bytes 1 | tf_op jit(solution)/shard_map/pallas_call | solution.py:281
  11.2 0.0 collective-permute-done.l2
  11.3 0.0 collective-permute-done.1.l1
  11.3 0.0 collective-permute-done.3.r1
  11.3 3.6 %shard_map.67 = f32[529,1,512]{2,1,0:T(1,128)} custom-call(bf16[64,529]{1,0:T(8,128)(2,1)S(1)} %collective-permute-done.l2, bf16[64,529]{1,0:T(8,128)(2,1)S(1)} %collective-permute-done.1.l1, bf16[529,128]{1,0:T(8,128)(2,1)S(1)} %collective-permute-done.3.r1, bf16[1937,256]{1,0:T(8,128)(2,1)S(1)} %get-tuple-element.18.t_ref, ...), custom_call_target="tpu_custom_call" | custom-call | flops 10000000000 | bytes 1 | tf_op jit(solution)/shard_map/pallas_call | solution.py:289
  (1 shorter events, 0.0 us)
Async XLA Ops:
  0.0 9.7 %collective-permute-start.2 = (bf16[529,128]{1,0:T(8,128)(2,1)}, bf16[529,128]{1,0:T(8,128)(2,1)S(1)}, u32[]{:S(2)}, u32[]{:S(2)}) collective-permute-start(bf16[529,128]{1,0:T(8,128)(2,1)} %bitcast.10), channel_id=1, source_target_pairs={{0,24},{4,28},{8,0},{12,4},{16,8},{20,12},{24,16},{28,20},{1,25},{... | collective-permute-start | bytes 406280 | tf_op jit(solution)/shard_map/ppermute | solution.py:30
  3.9 7.4 %collective-permute-start = (bf16[64,529]{1,0:T(8,128)(2,1)}, bf16[64,529]{1,0:T(8,128)(2,1)S(1)}, u32[]{:S(2)}, u32[]{:S(2)}) collective-permute-start(bf16[64,529]{1,0:T(8,128)(2,1)} %bitcast.12), channel_id=1, source_target_pairs={{0,2},{1,3},{2,0},{3,1},{4,6},{5,7},{6,4},{7,5},{8,10},{9,11},{10,... | collective-permute-start | bytes 203144 | tf_op jit(solution)/shard_map/ppermute | solution.py:30
  6.5 4.8 %collective-permute-start.1 = (bf16[64,529]{1,0:T(8,128)(2,1)}, bf16[64,529]{1,0:T(8,128)(2,1)S(1)}, u32[]{:S(2)}, u32[]{:S(2)}) collective-permute-start(bf16[64,529]{1,0:T(8,128)(2,1)} %bitcast.13), channel_id=1, source_target_pairs={{0,3},{1,0},{2,1},{3,2},{4,7},{5,4},{6,5},{7,6},{8,11},{9,8},{10,9... | collective-permute-start | bytes 203144 | tf_op jit(solution)/shard_map/ppermute | solution.py:30
  9.8 1.5 %collective-permute-start.3 = (bf16[529,128]{1,0:T(8,128)(2,1)S(1)}, bf16[529,128]{1,0:T(8,128)(2,1)S(1)}, u32[]{:S(2)}, u32[]{:S(2)}) collective-permute-start(bf16[529,128]{1,0:T(8,128)(2,1)S(1)} %shard_map.65._), channel_id=1, source_target_pairs={{0,4},{4,0},{8,12},{12,8},{16,20},{20,16},{24,28},{28,24},{1,5},{5... | collective-permute-start | bytes 406280 | tf_op jit(solution)/shard_map/ppermute | solution.py:280

commit v8 on v7

--- a/solution.py
+++ b/solution.py
@@ -182,14 +182,14 @@
 
 
 def far_right_kernel(r, slots_ref, near_ref, a0, b0, _, b_ref, p_ref, pick_ref, mask_ref, near_spread_ref, w_ref, spread_ref):
+    column_spread(near_ref[2], spread_ref)
+    right_panel(r, spread_ref, w_ref, b_ref)
+    for u in range(3):
+        put_rows(p_ref, None, product(((a0, b0),), u), u)
     for s in (1, 2):
         pick_ref[s - 1] = slot_pick(slots_ref[s : s + 1])
         mask_ref[s - 1] = slot_mask(slots_ref[s + 3 : s + 4])
     column_spread(near_ref[1], near_spread_ref)
-    column_spread(near_ref[2], spread_ref)
-    right_panel(r, spread_ref, w_ref, b_ref)
-    for u in range(3):
-        put_rows(p_ref, None, product(((a0, b0),), u), u)
 
 
 def last_kernel(l2, l1, r1, t_ref, pick_ref, mask_ref, spread_ref, b2, before_ref, out_hbm, a2, a1, b1, w_ref, p_ref, h_ref, o_ref, sems):

time: 15.1 us -> 15 us (level)
  transfers between devices with their start and end apart: 4 -> 4, of which waited for: 0 -> 1; matrix products, arithmetic and copies ran while one was open for 0% -> 0% of each run, Pallas kernels for 22% -> 21%
where the time goes in v8:
time: 15 us; the launch traced here: 14.9 us
  starting transfers between devices  7.9 us (53%)
  Pallas kernels  6.8 us (45%)
  waiting for transfers between devices  0.16 us (1%)
    ppermute x3, starting transfers between devices, from_behind(): lax.ppermute(value, axis, [(i, (i + by) % devices) for i in range(devices)])  7.83 us
    pallas_call x1, Pallas kernels, body(): call(last_kernel, 10 ** 10, shape(NB, 1, RB * CB), [VMEM] * 9, ANY, [pltp...  3.61 us
    pallas_call x1, Pallas kernels, body(): call(first_kernel, 1, (dense_left, dense_right, shape(NB, 128, dtype=BF16...  1.89 us
    pallas_call x1, Pallas kernels, body(): call(far_right_kernel, 10 ** 10, (dense_right, sums, shape(2, 4 * RB, SA,...  1.26 us
  transfers between devices with their start and end apart: 4, of which 1 were waited for; matrix products, arithmetic and copies ran while one was open for 0% of the time, Pallas kernels for 21%

profile of v8, /device:TPU:0, one launch (start us, length us, event | category | flops | bytes accessed | tf_op | source)
XLA Modules:
  0.0 14.9 jit_solution(7082002791137331647)
XLA Ops:
  0.0 3.9 %collective-permute-start.2 = (bf16[529,128]{1,0:T(8,128)(2,1)}, bf16[529,128]{1,0:T(8,128)(2,1)S(1)}, u32[]{:S(2)}, u32[]{:S(2)}) collective-permute-start(bf16[529,128]{1,0:T(8,128)(2,1)} %bitcast.10), channel_id=1, source_target_pairs={{0,24},{4,28},{8,0},{12,4},{16,8},{20,12},{24,16},{28,20},{1,25},{... | collective-permute-start | bytes 406280 | tf_op jit(solution)/shard_map/ppermute | solution.py:30
  3.9 2.6 %collective-permute-start = (bf16[64,529]{1,0:T(8,128)(2,1)}, bf16[64,529]{1,0:T(8,128)(2,1)S(1)}, u32[]{:S(2)}, u32[]{:S(2)}) collective-permute-start(bf16[64,529]{1,0:T(8,128)(2,1)} %bitcast.12), channel_id=1, source_target_pairs={{0,2},{1,3},{2,0},{3,1},{4,6},{5,7},{6,4},{7,5},{8,10},{9,11},{10,... | collective-permute-start | bytes 203144 | tf_op jit(solution)/shard_map/ppermute | solution.py:30
  6.5 1.3 %collective-permute-start.1 = (bf16[64,529]{1,0:T(8,128)(2,1)}, bf16[64,529]{1,0:T(8,128)(2,1)S(1)}, u32[]{:S(2)}, u32[]{:S(2)}) collective-permute-start(bf16[64,529]{1,0:T(8,128)(2,1)} %bitcast.13), channel_id=1, source_target_pairs={{0,3},{1,0},{2,1},{3,2},{4,7},{5,4},{6,5},{7,6},{8,11},{9,8},{10,9... | collective-permute-start | bytes 203144 | tf_op jit(solution)/shard_map/ppermute | solution.py:30
  7.8 1.9 %shard_map.64 = (bf16[368,1024]{1,0:T(8,128)(2,1)S(1)}, bf16[512,768]{1,0:T(8,128)(2,1)S(1)}, bf16[529,128]{1,0:T(8,128)(2,1)S(1)}, bf16[1937,256]{1,0:T(8,128)(...) custom-call(s32[1,4]{1,0:T(1,128)} %counts_hbm.1, s32[1,4,64]{2,1,0:T(4,128)} %rows_hbm.1, s32[1,4,64]{2,1,0:T(4,128)} %cols_hbm.1, ...), custom_call_target="tpu_custom_call" | custom-call | flops 1 | bytes 1 | tf_op jit(solution)/shard_map/pallas_call | solution.py:262
  9.7 0.0 collective-permute-done.2.r2.r
  9.8 0.1 collective-permute-start.3
  9.9 1.3 %shard_map.66 = (bf16[512,768]{1,0:T(8,128)(2,1)S(1)}, f32[6,384,128]{2,1,0:T(8,128)S(1)}, bf16[2,64,64]{2,1,0:T(8,128)(2,1)S(1)}, bf16[2,64,256]{2,1,0:T(8,128)(2,1)S(1)}, bf16[4,128,512]{2,1,0:T(8,128)(2,1)S(1)}) custom-call(bf16[529,128]{1,0:T(8,128)(2,1)S(1)} %collective-permute-done.2.r2.r, s32[8,64]{1,0:T(8,128)S(1)} %get-tuple-element.19.slots_ref, ...), custom_call_target="tpu_custom_call" | custom-call | flops 10000000000 | bytes 1 | tf_op jit(solution)/shard_map/pallas_call | solution.py:281
  11.1 0.0 collective-permute-done.l2
  11.1 0.1 collective-permute-done.1.l1
  11.3 0.0 collective-permute-done.3.r1
  11.3 3.6 %shard_map.67 = f32[529,1,512]{2,1,0:T(1,128)} custom-call(bf16[64,529]{1,0:T(8,128)(2,1)S(1)} %collective-permute-done.l2, bf16[64,529]{1,0:T(8,128)(2,1)S(1)} %collective-permute-done.1.l1, bf16[529,128]{1,0:T(8,128)(2,1)S(1)} %collective-permute-done.3.r1, bf16[1937,256]{1,0:T(8,128)(2,1)S(1)} %get-tuple-element.18.t_ref, ...), custom_call_target="tpu_custom_call" | custom-call | flops 10000000000 | bytes 1 | tf_op jit(solution)/shard_map/pallas_call | solution.py:289
  (1 shorter events, 0.0 us)
Async XLA Ops:
  0.0 9.7 %collective-permute-start.2 = (bf16[529,128]{1,0:T(8,128)(2,1)}, bf16[529,128]{1,0:T(8,128)(2,1)S(1)}, u32[]{:S(2)}, u32[]{:S(2)}) collective-permute-start(bf16[529,128]{1,0:T(8,128)(2,1)} %bitcast.10), channel_id=1, source_target_pairs={{0,24},{4,28},{8,0},{12,4},{16,8},{20,12},{24,16},{28,20},{1,25},{... | collective-permute-start | bytes 406280 | tf_op jit(solution)/shard_map/ppermute | solution.py:30
  3.9 7.2 %collective-permute-start = (bf16[64,529]{1,0:T(8,128)(2,1)}, bf16[64,529]{1,0:T(8,128)(2,1)S(1)}, u32[]{:S(2)}, u32[]{:S(2)}) collective-permute-start(bf16[64,529]{1,0:T(8,128)(2,1)} %bitcast.12), channel_id=1, source_target_pairs={{0,2},{1,3},{2,0},{3,1},{4,6},{5,7},{6,4},{7,5},{8,10},{9,11},{10,... | collective-permute-start | bytes 203144 | tf_op jit(solution)/shard_map/ppermute | solution.py:30
  6.5 4.8 %collective-permute-start.1 = (bf16[64,529]{1,0:T(8,128)(2,1)}, bf16[64,529]{1,0:T(8,128)(2,1)S(1)}, u32[]{:S(2)}, u32[]{:S(2)}) collective-permute-start(bf16[64,529]{1,0:T(8,128)(2,1)} %bitcast.13), channel_id=1, source_target_pairs={{0,3},{1,0},{2,1},{3,2},{4,7},{5,4},{6,5},{7,6},{8,11},{9,8},{10,9... | collective-permute-start | bytes 203144 | tf_op jit(solution)/shard_map/ppermute | solution.py:30
  9.8 1.5 %collective-permute-start.3 = (bf16[529,128]{1,0:T(8,128)(2,1)S(1)}, bf16[529,128]{1,0:T(8,128)(2,1)S(1)}, u32[]{:S(2)}, u32[]{:S(2)}) collective-permute-start(bf16[529,128]{1,0:T(8,128)(2,1)S(1)} %shard_map.65._), channel_id=1, source_target_pairs={{0,4},{4,0},{8,12},{12,8},{16,20},{20,16},{24,28},{28,24},{1,5},{5... | collective-permute-start | bytes 406280 | tf_op jit(solution)/shard_map/ppermute | solution.py:280

commit v9 on v8

--- a/solution.py
+++ b/solution.py
@@ -147,8 +147,8 @@
     moves = [
         pltpu.make_async_copy(s, d, sems.at[n])
         for n, (s, d) in enumerate((
-            (counts_hbm, counts), (rows_hbm, rows), (cols_hbm, cols), (kcols_hbm, kcols),
             (r_hbm, r_ref), (l_hbm, l_ref),
+            (kcols_hbm, kcols), (cols_hbm, cols), (rows_hbm, rows), (counts_hbm, counts),
         ))
     ]
     for move in moves:

time: 15 us -> 15 us (level)
  transfers between devices with their start and end apart: 4 -> 4, of which waited for: 1 -> 2; matrix products, arithmetic and copies ran while one was open for 0% -> 0% of each run, Pallas kernels for 21% -> 21%
where the time goes in v9:
time: 15 us; the launch traced here: 14.9 us
  starting transfers between devices  7.9 us (53%)
  Pallas kernels  6.75 us (45%)
  waiting for transfers between devices  0.2 us (1%)
    ppermute x3, starting transfers between devices, from_behind(): lax.ppermute(value, axis, [(i, (i + by) % devices) for i in range(devices)])  7.83 us
    pallas_call x1, Pallas kernels, body(): call(last_kernel, 10 ** 10, shape(NB, 1, RB * CB), [VMEM] * 9, ANY, [pltp...  3.61 us
    pallas_call x1, Pallas kernels, body(): call(first_kernel, 1, (dense_left, dense_right, shape(NB, 128, dtype=BF16...  1.85 us
    pallas_call x1, Pallas kernels, body(): call(far_right_kernel, 10 ** 10, (dense_right, sums, shape(2, 4 * RB, SA,...  1.26 us
  transfers between devices with their start and end apart: 4, of which 2 were waited for; matrix products, arithmetic and copies ran while one was open for 0% of the time, Pallas kernels for 21%

profile of v9, /device:TPU:0, one launch (start us, length us, event | category | flops | bytes accessed | tf_op | source)
XLA Modules:
  0.0 14.9 jit_solution(6359686537394691490)
XLA Ops:
  0.0 3.9 %collective-permute-start.2 = (bf16[529,128]{1,0:T(8,128)(2,1)}, bf16[529,128]{1,0:T(8,128)(2,1)S(1)}, u32[]{:S(2)}, u32[]{:S(2)}) collective-permute-start(bf16[529,128]{1,0:T(8,128)(2,1)} %bitcast.10), channel_id=1, source_target_pairs={{0,24},{4,28},{8,0},{12,4},{16,8},{20,12},{24,16},{28,20},{1,25},{... | collective-permute-start | bytes 406280 | tf_op jit(solution)/shard_map/ppermute | solution.py:30
  3.9 2.6 %collective-permute-start = (bf16[64,529]{1,0:T(8,128)(2,1)}, bf16[64,529]{1,0:T(8,128)(2,1)S(1)}, u32[]{:S(2)}, u32[]{:S(2)}) collective-permute-start(bf16[64,529]{1,0:T(8,128)(2,1)} %bitcast.12), channel_id=1, source_target_pairs={{0,2},{1,3},{2,0},{3,1},{4,6},{5,7},{6,4},{7,5},{8,10},{9,11},{10,... | collective-permute-start | bytes 203144 | tf_op jit(solution)/shard_map/ppermute | solution.py:30
  6.5 1.3 %collective-permute-start.1 = (bf16[64,529]{1,0:T(8,128)(2,1)}, bf16[64,529]{1,0:T(8,128)(2,1)S(1)}, u32[]{:S(2)}, u32[]{:S(2)}) collective-permute-start(bf16[64,529]{1,0:T(8,128)(2,1)} %bitcast.13), channel_id=1, source_target_pairs={{0,3},{1,0},{2,1},{3,2},{4,7},{5,4},{6,5},{7,6},{8,11},{9,8},{10,9... | collective-permute-start | bytes 203144 | tf_op jit(solution)/shard_map/ppermute | solution.py:30
  7.8 1.8 %shard_map.64 = (bf16[368,1024]{1,0:T(8,128)(2,1)S(1)}, bf16[512,768]{1,0:T(8,128)(2,1)S(1)}, bf16[529,128]{1,0:T(8,128)(2,1)S(1)}, bf16[1937,256]{1,0:T(8,128)(...) custom-call(s32[1,4]{1,0:T(1,128)} %counts_hbm.1, s32[1,4,64]{2,1,0:T(4,128)} %rows_hbm.1, s32[1,4,64]{2,1,0:T(4,128)} %cols_hbm.1, ...), custom_call_target="tpu_custom_call" | custom-call | flops 1 | bytes 1 | tf_op jit(solution)/shard_map/pallas_call | solution.py:262
  9.7 0.0 collective-permute-done.2.r2.r
  9.7 0.1 collective-permute-start.3
  9.8 1.3 %shard_map.66 = (bf16[512,768]{1,0:T(8,128)(2,1)S(1)}, f32[6,384,128]{2,1,0:T(8,128)S(1)}, bf16[2,64,64]{2,1,0:T(8,128)(2,1)S(1)}, bf16[2,64,256]{2,1,0:T(8,128)(2,1)S(1)}, bf16[4,128,512]{2,1,0:T(8,128)(2,1)S(1)}) custom-call(bf16[529,128]{1,0:T(8,128)(2,1)S(1)} %collective-permute-done.2.r2.r, s32[8,64]{1,0:T(8,128)S(1)} %get-tuple-element.19.slots_ref, ...), custom_call_target="tpu_custom_call" | custom-call | flops 10000000000 | bytes 1 | tf_op jit(solution)/shard_map/pallas_call | solution.py:281
  11.1 0.1 collective-permute-done.l2
  11.1 0.1 collective-permute-done.1.l1
  11.3 0.0 collective-permute-done.3.r1
  11.3 3.6 %shard_map.67 = f32[529,1,512]{2,1,0:T(1,128)} custom-call(bf16[64,529]{1,0:T(8,128)(2,1)S(1)} %collective-permute-done.l2, bf16[64,529]{1,0:T(8,128)(2,1)S(1)} %collective-permute-done.1.l1, bf16[529,128]{1,0:T(8,128)(2,1)S(1)} %collective-permute-done.3.r1, bf16[1937,256]{1,0:T(8,128)(2,1)S(1)} %get-tuple-element.18.t_ref, ...), custom_call_target="tpu_custom_call" | custom-call | flops 10000000000 | bytes 1 | tf_op jit(solution)/shard_map/pallas_call | solution.py:289
  (1 shorter events, 0.0 us)
Async XLA Ops:
  0.0 9.7 %collective-permute-start.2 = (bf16[529,128]{1,0:T(8,128)(2,1)}, bf16[529,128]{1,0:T(8,128)(2,1)S(1)}, u32[]{:S(2)}, u32[]{:S(2)}) collective-permute-start(bf16[529,128]{1,0:T(8,128)(2,1)} %bitcast.10), channel_id=1, source_target_pairs={{0,24},{4,28},{8,0},{12,4},{16,8},{20,12},{24,16},{28,20},{1,25},{... | collective-permute-start | bytes 406280 | tf_op jit(solution)/shard_map/ppermute | solution.py:30
  3.9 7.2 %collective-permute-start = (bf16[64,529]{1,0:T(8,128)(2,1)}, bf16[64,529]{1,0:T(8,128)(2,1)S(1)}, u32[]{:S(2)}, u32[]{:S(2)}) collective-permute-start(bf16[64,529]{1,0:T(8,128)(2,1)} %bitcast.12), channel_id=1, source_target_pairs={{0,2},{1,3},{2,0},{3,1},{4,6},{5,7},{6,4},{7,5},{8,10},{9,11},{10,... | collective-permute-start | bytes 203144 | tf_op jit(solution)/shard_map/ppermute | solution.py:30
  6.5 4.8 %collective-permute-start.1 = (bf16[64,529]{1,0:T(8,128)(2,1)}, bf16[64,529]{1,0:T(8,128)(2,1)S(1)}, u32[]{:S(2)}, u32[]{:S(2)}) collective-permute-start(bf16[64,529]{1,0:T(8,128)(2,1)} %bitcast.13), channel_id=1, source_target_pairs={{0,3},{1,0},{2,1},{3,2},{4,7},{5,4},{6,5},{7,6},{8,11},{9,8},{10,9... | collective-permute-start | bytes 203144 | tf_op jit(solution)/shard_map/ppermute | solution.py:30
  9.7 1.6 %collective-permute-start.3 = (bf16[529,128]{1,0:T(8,128)(2,1)S(1)}, bf16[529,128]{1,0:T(8,128)(2,1)S(1)}, u32[]{:S(2)}, u32[]{:S(2)}) collective-permute-start(bf16[529,128]{1,0:T(8,128)(2,1)S(1)} %shard_map.65._), channel_id=1, source_target_pairs={{0,4},{4,0},{8,12},{12,8},{16,20},{20,16},{24,28},{28,24},{1,5},{5... | collective-permute-start | bytes 406280 | tf_op jit(solution)/shard_map/ppermute | solution.py:280
